TPU v7x, 512 devices: a whole 4x4x16 slice. The times are simulated.
512 devices in a mesh: rep: 8 (over z_lo), sp: 8 (over x, core), tp: 8 (over z_hi, y).
Axes of the slice: x: 4, y: 4, z: 16 (z_hi: 2, z_lo: 8; z = z_hi * 8 + z_lo), core: 2. Of those that a mesh axis runs over, the one named last changes fastest.
Arguments:
- latents: bfloat16 [8, 1, 1536, 5120], P('rep', None, 'sp'), may hold values from -6 to 6
- timesteps: int32 [8], P('rep'), may hold values from 0 to 49
- mod_table: float32 [50, 2, 5120], replicated, may hold values from -2 to 2
- w_query: bfloat16 [5120, 3072], P('rep', 'tp'), may hold values from -1 to 1
- w_key: bfloat16 [5120, 3072], P('rep', 'tp'), may hold values from -1 to 1
- w_value: bfloat16 [5120, 3072], P('rep', 'tp'), may hold values from -0.078125 to 0.078125
- q_gain: float32 [3072], replicated, may hold values from 0 to 4
- k_gain: float32 [3072], replicated, may hold values from 0 to 4
Outputs:
- context: bfloat16 [8, 1, 1536, 3072], P('rep', None, 'sp', 'tp')
All inputs are finite; a program needn't handle non-finite values.
Results may differ from a plain program's by a relative error of at most 0.0057.
Values may be sent and summed in bfloat16 or wider, within the bound.
A program may use at most 64 MiB of HBM per device.

v0:
```python
import jax
import jax.numpy as jnp
from jax import lax
from jax.sharding import PartitionSpec as P

HEAD_DIM = 128


def local(latents, timesteps, mod_table, w_query, w_key, w_value, q_gain, k_gain):
    clips = latents.shape[1]
    seq_dev = latents.shape[2]
    width = latents.shape[3]
    steps_total = mod_table.shape[0]
    onehot = (lax.iota(jnp.int32, steps_total) == timesteps[0]).astype(jnp.float32)
    modulation = jnp.dot(
        onehot, mod_table.reshape(steps_total, 2 * width), precision=lax.Precision.HIGHEST
    ).reshape(2, width)
    values = latents[0].reshape(clips * seq_dev, width).astype(jnp.float32)
    center = values - jnp.mean(values, axis=-1, keepdims=True)
    spread = jnp.mean(center * center, axis=-1, keepdims=True)
    normed = (center * lax.rsqrt(spread + 1e-06) * (1.0 + modulation[1]) + modulation[0]).astype(
        jnp.bfloat16
    )
    stacked = jnp.concatenate([w_query, w_key, w_value], axis=1)
    projected = jnp.dot(
        normed,
        lax.all_gather(stacked, "rep", axis=0, tiled=True),
        preferred_element_type=jnp.float32,
    )
    cols_tp = w_query.shape[1]
    projected_half = projected.astype(jnp.bfloat16).reshape(clips, seq_dev, 3, cols_tp)
    rows_full = lax.all_to_all(projected_half, "tp", split_axis=1, concat_axis=3, tiled=True)
    inner = rows_full.shape[3]
    row_count = rows_full.shape[1]
    pair = rows_full[:, :, 0:2].astype(jnp.float32)
    gains = jnp.stack([q_gain, k_gain])
    pair_normed = (
        pair * gains * lax.rsqrt(jnp.mean(pair * pair, axis=-1, keepdims=True) + 1e-06)
    ).astype(jnp.bfloat16)
    packed = jnp.concatenate([pair_normed, rows_full[:, :, 2:3]], axis=2)
    packed = packed.reshape(clips, row_count, 3, inner // HEAD_DIM, HEAD_DIM)
    inverse_root = 1.0 / jnp.sqrt(jnp.float32(HEAD_DIM))
    block = lax.all_to_all(packed, "sp", split_axis=3, concat_axis=1, tiled=True)
    query = block[:, :, 0]
    keys = block[:, :, 1]
    vals = block[:, :, 2]
    items = query.shape[0]
    queries = query.shape[1]
    heads = query.shape[2]
    peak = jnp.full((items, heads, queries), -1e30, jnp.float32)
    accum = jnp.zeros((items, queries, heads, HEAD_DIM), jnp.float32)
    key_piece = lax.all_gather(keys, "tp", axis=1, tiled=True)
    val_piece = lax.all_gather(vals, "tp", axis=1, tiled=True)
    scores = (
        jnp.einsum("nqhd,nkhd->nhqk", query, key_piece, preferred_element_type=jnp.float32)
        * inverse_root
    )
    new_peak = jnp.maximum(peak, jnp.max(scores, axis=-1))
    fade = jnp.exp(peak - new_peak)
    weights = jnp.exp(scores - new_peak[..., None])
    total = jnp.sum(weights, axis=-1)
    rounded = weights.astype(jnp.bfloat16)
    update = jnp.einsum("nhqk,nkhd->nqhd", rounded, val_piece, preferred_element_type=jnp.float32)
    accum = accum * jnp.swapaxes(fade, 1, 2)[..., None] + update
    peak, total, accum = (new_peak, total, accum)
    attended = (accum / jnp.swapaxes(total, 1, 2)[..., None]).astype(jnp.bfloat16)
    flat = attended.reshape(clips, attended.shape[1], attended.shape[2] * HEAD_DIM)
    restored = lax.all_to_all(
        lax.all_to_all(flat, "sp", split_axis=1, concat_axis=2, tiled=True),
        "tp",
        split_axis=2,
        concat_axis=1,
        tiled=True,
    )
    return restored[None]


def solution(mesh):
    return jax.shard_map(
        local,
        mesh=mesh,
        in_specs=(
            P("rep", None, "sp", None),
            P("rep"),
            P(),
            P("rep", "tp"),
            P("rep", "tp"),
            P("rep", "tp"),
            P(),
            P(),
        ),
        out_specs=P("rep", None, "sp", "tp"),
        check_vma=False,
    )
```

profile of v0, /device:TPU:1, one launch (start us, length us, event | category | flops | bytes accessed | tf_op | source)
XLA Modules:
  0.0 566.4 jit_solution(15324336586350095896)
XLA Ops:
  6.5 2.8 pad_maximum_fusion
  9.4 0.8 pad.7
  10.1 0.7 copy.45
  12.7 0.9 fusion.42
  13.6 245.7 %all-gather.6.cloned.1.call-done = bf16[5120,1152]{1,0:T(8,128)(2,1)} async-done(((bf16[640,1152]{1,0:T(8,128)(2,1)}), bf16[5120,1152]{1,0:T(8,128)(2,1)}) %all-gather.6.cloned.1.call-update) | async-done | bytes 11796496 | tf_op jit(solution)/shard_map/all_gather | solution.py:27
  259.3 7.1 %convolution_convert_fusion = bf16[192,1152]{1,0:T(8,128)(2,1)S(1)} fusion(bf16[5120,1152]{1,0:T(8,128)(2,1)} %all-gather.6.cloned.1.call-done, bf16[1,1,192,5120]{3,2,1,0:T(8,128)(2,1)S(1)} %copy-done, f32[5120]{0:T(1024)S(1)} %get-tuple-element.8, f32[5120]{0:T(1024)S(1)} %get-tuple-element.7, f32[192]{0:T(256)S(1)} %add_rsqrt_fusion.1, ...), kind=kOutput, calls=%fused_computation.13 | convolution fusion | flops 2271043584 | bytes 14247424 | tf_op jit(solution)/shard_map/dot_general | solution.py:25
  266.4 0.9 reshape.108
  267.3 9.0 %all-to-all-start = ((bf16[1,192,3,384]{3,2,0,1:T(4,128)(2,1)}), bf16[1,192,3,384]{3,2,0,1:T(4,128)(2,1)S(1)}, u32[]{:S(2)}, u32[]{:S(2)}) async-start(bf16[1,192,3,384]{3,2,0,1:T(4,128)(2,1)} %bitcast.4), calls=%async_computation | async-start | bytes 1179648 | tf_op jit(solution)/shard_map/all_to_all | solution.py:32
  276.5 17.5 %all-to-all-done = bf16[1,192,3,384]{3,2,0,1:T(4,128)(2,1)S(1)} async-done(((bf16[1,192,3,384]{3,2,0,1:T(4,128)(2,1)}), bf16[1,192,3,384]{3,2,0,1:T(4,128)(2,1)S(1)}, u32[]{:S(2)}, u32[]{:S(2)}) %all-to-all-start) | async-done | bytes 442400 | tf_op jit(solution)/shard_map/all_to_all | solution.py:32
  294.7 20.9 %all_to_all.69 = bf16[1,24,3,24,128]{4,1,2,0,3:T(8,128)(2,1)S(1)} all-to-all(bf16[1,24,3,24,128]{4,1,2,0,3:T(8,128)(2,1)S(1)} %copy_bitcast_fusion), channel_id=1, replica_groups=mesh['rep'=8,'sp'=8,'tp'=8] {'sp'}, dimensions={3} | all-to-all | bytes 884736 | tf_op jit(solution)/shard_map/all_to_all | solution.py:43
  315.7 0.8 copy-done.2
  316.5 0.7 fusion.47
  318.0 95.4 %all-gather.8.cloned.1.call-done = bf16[1,1536,1,3,128]{4,1,3,2,0:T(8,128)(2,1)} async-done(((bf16[1,192,1,3,128]{4,1,3,2,0:T(8,128)(2,1)}), bf16[1,1536,1,3,128]{4,1,3,2,0:T(8,128)(2,1)}) %all-gather.8.cloned.1.call-update) | async-done | bytes 1179664 | tf_op jit(solution)/shard_map/all_gather | solution.py:52
  413.3 2.1 fusion.48
  416.1 86.0 %all-gather.10.cloned.1.call-done = bf16[1,1536,1,3,128]{4,1,3,2,0:T(8,128)(2,1)} async-done(((bf16[1,192,1,3,128]{4,1,3,2,0:T(8,128)(2,1)}), bf16[1,1536,1,3,128]{4,1,3,2,0:T(8,128)(2,1)}) %all-gather.10.cloned.1.call-update) | async-done | bytes 1179664 | tf_op jit(solution)/shard_map/all_gather | solution.py:53
  502.0 2.0 fusion.34
  504.9 1.5 reduce.6
  506.4 11.5 %all_to_all.70 = bf16[8,2,4608]{2,1,0:T(2,128)(2,1)S(1)} all-to-all(bf16[8,2,4608]{2,1,0:T(2,128)(2,1)S(1)} %reshape.121), channel_id=1, replica_groups=mesh['rep'=8,'sp'=8,'tp'=8] {'sp'}, dimensions={0} | all-to-all | bytes 294912 | tf_op jit(solution)/shard_map/all_to_all | solution.py:69
  518.1 1.9 copy.39
  520.0 17.0 %reduce.7 = bf16[3072,24]{1,0:T(8,128)(2,1)S(1)} reduce(bf16[3072,1,24]{2,1,0:T(2,128)(2,1)S(1)} %bitcast.110, bf16[]{:T(256)} %broadcast.79), dimensions={1}, to_apply=%bitcast.96.reduce_sub_computation | reduce | bytes 294914
  537.0 1.0 reshape.123
  538.0 17.6 %all_to_all.71 = bf16[8,2,4608]{2,1,0:T(2,128)(2,1)S(1)} all-to-all(bf16[8,2,4608]{2,1,0:T(2,128)(2,1)S(1)} %reshape.123), channel_id=1, replica_groups=mesh['rep'=8,'sp'=8,'tp'=8] {'tp'}, dimensions={0} | all-to-all | bytes 294912 | tf_op jit(solution)/shard_map/all_to_all | solution.py:68
  555.6 2.1 reshape.124
  557.7 1.4 copy.40
  (42 shorter events, 5.2 us)
Async XLA Ops:
  6.5 2.8 copy-start.1
  6.5 252.7 %all-gather.6.cloned.1.call-start = ((), (), s32[]{:S(2)}) async-start(), calls=%async_computation.4 | async-start | bytes 13271040 | tf_op jit(solution)/shard_map/all_gather | solution.py:27
  10.1 1.5 copy-start
  259.3 17.2 %copy-start.3 = (f32[3072]{0:T(1024)S(1)}, f32[3072]{0:T(1024)}, u32[]{:S(2)}) copy-start(f32[3072]{0:T(1024)} %param.15) | copy-start | bytes 36868
  259.3 17.2 %copy-start.4 = (f32[3072]{0:T(1024)S(1)}, f32[3072]{0:T(1024)}, u32[]{:S(2)}) copy-start(f32[3072]{0:T(1024)} %param.14) | copy-start | bytes 36868
  267.3 26.6 %all-to-all-start = ((bf16[1,192,3,384]{3,2,0,1:T(4,128)(2,1)}), bf16[1,192,3,384]{3,2,0,1:T(4,128)(2,1)S(1)}, u32[]{:S(2)}, u32[]{:S(2)}) async-start(bf16[1,192,3,384]{3,2,0,1:T(4,128)(2,1)} %bitcast.4), calls=%async_computation | async-start | bytes 1179648 | tf_op jit(solution)/shard_map/all_to_all | solution.py:32
  276.4 137.0 %all-gather.8.cloned.1.call-start = ((), (), s32[]{:S(2)}) async-start(), calls=%async_computation.5 | async-start | bytes 1327104 | tf_op jit(solution)/shard_map/all_gather | solution.py:52
  315.7 0.8 copy-start.2
  317.2 184.8 %all-gather.10.cloned.1.call-start = ((), (), s32[]{:S(2)}) async-start(), calls=%async_computation.6 | async-start | bytes 1327104 | tf_op jit(solution)/shard_map/all_gather | solution.py:53
Sparse Core Ops, SparseCore 0:
  9.5 249.7 all-gather.5
  317.3 95.9 all-gather.7
  416.5 85.5 all-gather.9
where the time goes:
time: 567 us; the launch traced here: 566 us
  waiting for transfers between devices  445 us (78%)
  blocking collectives  50 us (9%)
  other arithmetic  23.3 us (4%)
  between operations  14 us (2%)
  local copies, waits for them, and re-layouts  12.6 us (2%)
  matrix products  12.1 us (2%)
  starting transfers between devices  9.1 us (2%)
    all_gather x1, waiting for transfers between devices, local(): lax.all_gather(stacked, 'rep', axis=0, tiled=True)  246 us
    all_gather x1, waiting for transfers between devices, local(): key_piece = lax.all_gather(keys, 'tp', axis=1, tiled=True)  95.4 us
    all_gather x1, waiting for transfers between devices, local(): val_piece = lax.all_gather(vals, 'tp', axis=1, tiled=True)  86 us
    all_to_all x1, blocking collectives, local(): lax.all_to_all(packed, 'sp', split_axis=3, concat_axis=1, tiled=True)  20.9 us
    unnamed x2, other arithmetic  18.5 us
    all_to_all x1, blocking collectives, local(): lax.all_to_all(lax.all_to_all(flat, 'sp', split_axis=1, concat_axis=2, ti...  17.6 us
    all_to_all x1, waiting for transfers between devices, local(): lax.all_to_all(projected_half, 'tp', split_axis=1, concat_axis=3, tiled=T...  17.5 us
    all_to_all x1, blocking collectives, local(): lax.all_to_all(flat, 'sp', split_axis=1, concat_axis=2, tiled=True)  11.5 us
  transfers between devices with their start and end apart: 4, of which 4 were waited for; matrix products, arithmetic and copies ran while one was open for 1% of the time, Pallas kernels for 0%

commit v1 on v0

v1 whole, which is shorter than its diff:
```python
import jax
import jax.numpy as jnp
from jax import lax
from jax.sharding import PartitionSpec as P

HEAD_DIM = 128


def local(latents, timesteps, mod_table, w_query, w_key, w_value, q_gain, k_gain):
    seq_dev, width = latents.shape[2], latents.shape[3]
    cols = w_query.shape[1]
    heads = cols // HEAD_DIM
    sp = lax.axis_size("sp")
    part = w_query.shape[0] // sp
    stacked = jnp.concatenate(
        [lax.dynamic_slice_in_dim(w, lax.axis_index("sp") * part, part, 0) for w in (w_query, w_key, w_value)],
        axis=1,
    )
    weights = lax.all_gather(stacked, ("rep", "sp"), axis=0, tiled=True)

    modulation = lax.dynamic_index_in_dim(mod_table, timesteps[0], 0, keepdims=False)
    values = latents.reshape(seq_dev, width).astype(jnp.float32)
    center = values - jnp.mean(values, axis=-1, keepdims=True)
    spread = jnp.mean(center * center, axis=-1, keepdims=True)
    normed = (center * lax.rsqrt(spread + 1e-06) * (1.0 + modulation[1]) + modulation[0]).astype(jnp.bfloat16)

    projected = jnp.dot(normed, weights, preferred_element_type=jnp.float32).astype(jnp.bfloat16)
    query, keys, vals = (projected[:, i * cols : (i + 1) * cols] for i in range(3))
    pair = jnp.stack([query, keys]).astype(jnp.float32)
    inner = cols * lax.axis_size("tp")
    square = lax.psum(jnp.sum(pair * pair, axis=-1), "tp") / inner
    start = lax.axis_index("tp") * cols
    gains = jnp.stack([lax.dynamic_slice_in_dim(g, start, cols, 0) for g in (q_gain, k_gain)])
    pair = (pair * gains[:, None, :] * lax.rsqrt(square[..., None] + 1e-06)).astype(jnp.bfloat16)

    both = lax.all_gather(jnp.stack([pair[1], vals]), "sp", axis=1, tiled=True)
    qh = pair[0].reshape(seq_dev, heads, HEAD_DIM)
    kh = both[0].reshape(-1, heads, HEAD_DIM)
    vh = both[1].reshape(-1, heads, HEAD_DIM)
    scores = jnp.einsum("qhd,khd->hqk", qh, kh, preferred_element_type=jnp.float32) / jnp.sqrt(jnp.float32(HEAD_DIM))
    soft = jnp.exp(scores - jnp.max(scores, axis=-1, keepdims=True))
    total = jnp.sum(soft, axis=-1)
    out = jnp.einsum("hqk,khd->qhd", soft.astype(jnp.bfloat16), vh, preferred_element_type=jnp.float32)
    out = (out / jnp.swapaxes(total, 0, 1)[..., None]).astype(jnp.bfloat16)
    return out.reshape(1, 1, seq_dev, cols)


def solution(mesh):
    return jax.shard_map(
        local,
        mesh=mesh,
        in_specs=(
            P("rep", None, "sp", None),
            P("rep"),
            P(),
            P("rep", "tp"),
            P("rep", "tp"),
            P("rep", "tp"),
            P(),
            P(),
        ),
        out_specs=P("rep", None, "sp", "tp"),
        check_vma=False,
    )
```

time: 567 us -> 238 us (0.42)
  waiting for transfers between devices: 445 us -> 162 us
  other arithmetic: 23.3 us -> 5.86 us
  blocking collectives: 50 us -> 37.8 us
  starting transfers between devices: 9.1 us -> 0.04 us
    all_gather x3 -> x2, waiting for transfers between devices: 427 us -> 162 us  [the longest x1 134 us: local(): weights = lax.all_gather(stacked, ('rep', 'sp'), axis=0, tiled=True)]
    all_to_all x3 -> x0, blocking collectives: 50 us -> none  [the longest x1 20.9 us: local(): lax.all_to_all(packed, 'sp', split_axis=3, concat_axis=1, tiled=True)]
    psum x0 -> x1, blocking collectives: none -> 37.8 us  [local(): square = lax.psum(jnp.sum(pair * pair, axis=-1), 'tp') / inner]
    unnamed x2 -> x0, other arithmetic: 18.5 us -> none
    all_to_all x1 -> x0, waiting for transfers between devices: 17.5 us -> none  [local(): lax.all_to_all(projected_half, 'tp', split_axis=1, concat_axis=3, tiled=T...]
    all_to_all x1 -> x0, starting transfers between devices: 9.02 us -> none  [local(): lax.all_to_all(projected_half, 'tp', split_axis=1, concat_axis=3, tiled=T...]
    dot_general x4 -> x3, matrix products: 12.1 us -> 8.57 us  [the longest x1 7.12 us: local(): jnp.dot(normed, weights, preferred_element_type=jnp.float32)]
  transfers between devices with their start and end apart: 4 -> 2, of which waited for: 4 -> 2; matrix products, arithmetic and copies ran while one was open for 1% -> 2% of each run, Pallas kernels for 0% -> 0%
where the time goes in v1:
time: 238 us
  waiting for transfers between devices  162 us (68%)
  blocking collectives  37.8 us (16%)
  between operations  14.1 us (6%)
  local copies, waits for them, and re-layouts  9.59 us (4%)
  matrix products  8.57 us (4%)
  other arithmetic  5.86 us (2%)
    all_gather x1, waiting for transfers between devices, local(): weights = lax.all_gather(stacked, ('rep', 'sp'), axis=0, tiled=True)  134 us
    psum x1, blocking collectives, local(): square = lax.psum(jnp.sum(pair * pair, axis=-1), 'tp') / inner  37.8 us
    all_gather x1, waiting for transfers between devices, local(): both = lax.all_gather(jnp.stack([pair[1], vals]), 'sp', axis=1, tiled=True)  28.3 us
    dot_general x1, matrix products, local(): jnp.dot(normed, weights, preferred_element_type=jnp.float32)  7.12 us
  transfers between devices with their start and end apart: 2, of which 2 were waited for; matrix products, arithmetic and copies ran while one was open for 2% of the time, Pallas kernels for 0%

profile of v1, /device:TPU:1, one launch (start us, length us, event | category | flops | bytes accessed | tf_op | source)
XLA Modules:
  0.0 238.0 jit_solution(6308983607649074845)
XLA Ops:
  6.5 1.0 copy-done
  7.6 0.9 constant_dynamic-slice_fusion
  8.4 0.7 pad_maximum_fusion.2
  9.2 0.0 all-gather.5.cloned.1.call-start
  9.9 0.8 dynamic_slice.23
  10.7 0.8 dynamic_slice.24
  11.4 1.9 convert_reduce_fusion
  13.4 0.7 fusion.3
  14.0 0.9 dynamic-slice_add_fusion
  14.9 133.7 %all-gather.3.cloned.1.call-done = bf16[5120,1152]{1,0:T(8,128)(2,1)} async-done(((bf16[80,1152]{1,0:T(8,128)(2,1)}), bf16[5120,1152]{1,0:T(8,128)(2,1)}) %all-gather.3.cloned.1.call-update) | async-done | bytes 11796496 | tf_op jit(solution)/shard_map/all_gather | solution.py:19
  148.7 7.1 %convolution_convert_fusion = bf16[192,1152]{1,0:T(8,128)(2,1)S(1)} fusion(bf16[5120,1152]{1,0:T(8,128)(2,1)} %all-gather.3.cloned.1.call-done, bf16[1,1,192,5120]{3,2,1,0:T(8,128)(2,1)S(1)} %copy-done.1, f32[5120]{0:T(1024)S(1)} %bitcast.44, f32[5120]{0:T(1024)S(1)} %bitcast.43, f32[192]{0:T(256)S(1)} %add_rsqrt_fusion.1, f32[192]{0:T(256)S(1)} %broadcast_multiply_fusion), kind=kOutput, calls=%fused_computation.13 | convolution fusion | flops 2271043584 | bytes 14247424 | tf_op jit(solution)/shard_map/dot_general | solution.py:27
  155.8 0.2 fusion.28
  156.0 37.8 %psum.7 = f32[2,192]{1,0:T(2,128)S(1)} all-reduce(f32[2,192]{1,0:T(2,128)S(1)} %fusion.28), channel_id=1, replica_groups=mesh['rep'=8,'sp'=8,'tp'=8] {'tp'}, use_global_device_ids=true, to_apply=%region_3.4 | all-reduce | flops 384 | bytes 3072 | tf_op jit(solution)/shard_map/psum | solution.py:31
  193.8 0.1 fusion.27
  193.9 0.8 pad_maximum_fusion.1
  194.8 28.3 %all-gather.5.cloned.1.call-done = bf16[2,1536,384]{2,1,0:T(8,128)(2,1)} async-done(((bf16[2,192,384]{2,1,0:T(8,128)(2,1)}), bf16[2,1536,384]{2,1,0:T(8,128)(2,1)}) %all-gather.5.cloned.1.call-update) | async-done | bytes 2359312 | tf_op jit(solution)/shard_map/all_gather | solution.py:36
  223.0 2.9 %fusion.30 = (bf16[1,1536,384]{2,1,0:T(8,128)(2,1)S(1)}, bf16[1,1536,384]{2,1,0:T(8,128)(2,1)}) fusion(bf16[2,1536,384]{2,1,0:T(8,128)(2,1)} %all-gather.5.cloned.1.call-done), kind=kLoop, calls=%fused_computation.44 | loop fusion | bytes 4718592 | tf_op jit(solution)/shard_map/slice | solution.py:38
  225.9 0.6 copy.13
  226.6 1.6 copy.12
  228.1 0.7 fusion.32
  228.8 0.6 fusion.7
  229.5 0.7 fusion.23
  230.2 0.1 copy.17
  230.4 0.8 reshape.34
  (16 shorter events, 0.2 us)
Async XLA Ops:
  6.5 1.0 copy-start
  6.5 6.8 %copy-start.1 = (bf16[1,1,192,5120]{3,2,1,0:T(8,128)(2,1)S(1)}, bf16[1,1,192,5120]{3,2,1,0:T(8,128)(2,1)}, u32[]{:S(2)}) copy-start(bf16[1,1,192,5120]{3,2,1,0:T(8,128)(2,1)} %param.8) | copy-start | bytes 5898244
  6.5 142.1 %all-gather.3.cloned.1.call-start = ((), (), s32[]{:S(2)}) async-start(), calls=%async_computation | async-start | bytes 11980800 | tf_op jit(solution)/shard_map/all_gather | solution.py:19
  9.2 213.9 %all-gather.5.cloned.1.call-start = ((), (), s32[]{:S(2)}) async-start(), calls=%async_computation.1 | async-start | bytes 2654208 | tf_op jit(solution)/shard_map/all_gather | solution.py:36
Sparse Core Ops, SparseCore 0:
  9.5 139.1 all-gather.2
  194.8 28.1 all-gather.4

commit v2 on v1

v2 whole, which is shorter than its diff:
```python
import functools

import jax
import jax.numpy as jnp
from jax import lax
from jax.experimental import pallas as pl
from jax.experimental.pallas import tpu as pltpu
from jax.sharding import PartitionSpec as P

HEAD_DIM = 128
SKEW = 2
LAG_X = 1
LAG_F = 2
MESH = pl.DeviceIdType.MESH


def dot(a, b, dims=((1,), (0,)), precision=None):
    return lax.dot_general(a, b, (dims, ((), ())), precision=precision, preferred_element_type=jnp.float32)


def kernel(
    sizes,
    steps_ref, latents_hbm, table_hbm, wk_hbm, wv_hbm, wq_hbm, kgain_ref, qgain_ref,
    out_ref,
    wbuf, latents, table, modulation, normed, acc, kvbuf, qbuf, sums,
    local_sem, zrecv, zrest, xrecv, srecv, kvrecv, kvsib, sumrecv, zsend, xsend, ssend, sumsend,
):
    nz, nx, nt = sizes
    r, s, tp = lax.axis_index("rep"), lax.axis_index("sp"), lax.axis_index("tp")
    x, c = s // 2, s % 2
    step = 1 - 2 * c
    fore, back = (x + step + nx) % nx, (x - step + nx) % nx
    base = c * nx
    mine, of_back, of_fore, of_far = base + x, base + back, base + fore, base + (x + 2) % nx
    to_fore, to_back, to_core = {"sp": fore * 2 + c}, {"sp": back * 2 + c}, {"sp": s + 1 - 2 * c}
    up, down = {"rep": r + 1}, {"rep": r - 1}
    whbm = (wk_hbm, wv_hbm, wq_hbm)
    rows, width = latents.shape
    cols = kvbuf.shape[3]
    heads = cols // HEAD_DIM

    def send(src, dst, send_sem, recv_sem, where):
        pltpu.make_async_remote_copy(src, dst, send_sem, recv_sem, device_id=where, device_id_type=MESH).start()

    def arrived(ref, recv_sem):
        pltpu.make_async_remote_copy(ref, ref, xsend.at[0], recv_sem, device_id=to_fore, device_id_type=MESH).wait_recv()

    def sent(ref, send_sem):
        pltpu.make_async_remote_copy(ref, ref, send_sem, sumrecv.at[0], device_id=to_fore, device_id_type=MESH).wait_send()

    loads = [pltpu.make_async_copy(latents_hbm, latents, local_sem.at[0]),
             pltpu.make_async_copy(table_hbm, table, local_sem.at[1])]
    loads += [pltpu.make_async_copy(whbm[m], wbuf.at[m, r], local_sem.at[2 + m]) for m in range(3)]
    for load in loads:
        load.start()

    barrier = pltpu.get_barrier_semaphore()

    def greet(where):
        pl.semaphore_signal(barrier, inc=1, device_id=where, device_id_type=MESH)

    for where in (to_fore, to_back, to_core):
        greet(where)
    for i in range(1, nt):
        greet({"tp": (tp + i) % nt})
    pl.when(r < nz - 1)(lambda: greet(up))
    pl.when(r > 0)(lambda: greet(down))
    inside = jnp.logical_and(r > 0, r < nz - 1)
    pl.when(inside)(lambda: pl.semaphore_wait(barrier, 4 + nt))
    pl.when(jnp.logical_not(inside))(lambda: pl.semaphore_wait(barrier, 3 + nt))

    def both_ways(action):
        pl.when(r < nz - 1)(lambda: action(up, 0))
        pl.when(r > 0)(lambda: action(down, 1))

    def send_own(m):
        both_ways(lambda where, way: send(whbm[m].at[mine], wbuf.at[m, r, mine], zsend.at[m], zrecv.at[m, r], where))

    def send_rest(m):
        def one(where, way):
            for i in range(1, nx):
                piece = base + (x + i) % nx
                send(whbm[m].at[piece], wbuf.at[m, r, piece], zsend.at[m], zrest.at[m, way], where)
        both_ways(one)

    def over_sources(k, least, action):
        pl.when(jnp.logical_and(k >= least, r - k >= 0))(lambda: action(r - k, 0))
        pl.when(jnp.logical_and(k >= least, r + k <= nz - 1))(lambda: action(r + k, 1))

    def z_event(k, m):
        def one(src, way):
            piece = wbuf.at[m, src, mine]
            arrived(piece, zrecv.at[m, src])
            if way == 0:
                pl.when(r < nz - 1)(lambda: send(piece, piece, zsend.at[m], zrecv.at[m, src], up))
            else:
                pl.when(r > 0)(lambda: send(piece, piece, zsend.at[m], zrecv.at[m, src], down))

            @pl.when(k >= 2)
            def _():
                send(piece, piece, xsend.at[m], xrecv.at[0, m, src], to_fore)
                send(piece, piece, xsend.at[m], xrecv.at[1, m, src], to_back)
        over_sources(k, 1, one)

    def x_event(k, m):
        def one(src, way):
            piece = wbuf.at[m, src, of_back]
            arrived(piece, xrecv.at[0, m, src])
            send(piece, piece, xsend.at[m], xrecv.at[2, m, src], to_fore)
        over_sources(k, 2, one)

    def to_sibling(m, src):
        block = wbuf.at[m, src, pl.ds(base, nx)]
        send(block, block, ssend.at[m], srecv.at[m], to_core)

    def f_event(k, m):
        def one(src, way):
            arrived(wbuf.at[m, src, of_fore], xrecv.at[1, m, src])
            arrived(wbuf.at[m, src, of_far], xrecv.at[2, m, src])
            to_sibling(m, src)
        over_sources(k, 2, one)

    def rest_event(m):
        def one(src, way):
            arrived(wbuf.at[m, src, pl.ds(0, nx - 1)], zrest.at[m, way])
            to_sibling(m, src)
        over_sources(1, 1, one)

    def slot(t):
        for m in range(3):
            z_event(t - SKEW * m, m)
        for m in range(3):
            x_event(t - SKEW * m - LAG_X, m)
        for m in range(3):
            f_event(t - SKEW * m - LAG_F, m)

    def slots(first, end, extra=None):
        @pl.loop(first, end)
        def _(t):
            slot(t)
            if extra is not None:
                extra(t - first)

    norm_rows = rows // 6 if rows % 96 == 0 else rows // 2

    def norm_block(i):
        at = pl.ds(pl.multiple_of(i * norm_rows, norm_rows), norm_rows)
        values = latents[at, :].astype(jnp.float32)
        center = values - jnp.mean(values, axis=-1, keepdims=True)
        spread = jnp.mean(center * center, axis=-1, keepdims=True)
        scaled = center * lax.rsqrt(spread + 1e-06) * modulation[1:2, :] + modulation[0:1, :]
        normed[at, :] = scaled.astype(jnp.bfloat16)

    def project(m):
        arrived(wbuf.at[m, pl.ds(0, nz - 1), pl.ds(0, nx)], srecv.at[m])
        depth = width // nz
        acc[...] = jnp.zeros_like(acc)

        @pl.loop(0, nz)
        def _(src):
            at = pl.ds(pl.multiple_of(src * depth, HEAD_DIM), depth)
            acc[...] += dot(normed[:, at], wbuf[m, src].reshape(depth, cols))
        return acc[...].astype(jnp.bfloat16)

    def send_sums(i, values):
        wide = values.astype(jnp.float32)
        square = dot(jnp.ones((8, cols), jnp.float32), wide * wide, ((1,), (1,)), lax.Precision.HIGHEST)
        sums[i, tp] = jnp.zeros(sums.shape[2:], jnp.float32)
        sums[i, tp, :, 0:rows] = square[0:1]
        for j in range(1, nt):
            send(sums.at[i, tp], sums.at[i, tp], sumsend.at[i], sumrecv.at[i], {"tp": (tp + j) % nt})

    def normalise(i, values, gain_ref):
        arrived(sums.at[i, pl.ds(0, nt - 1)], sumrecv.at[i])
        total = sums[i, 0]
        for j in range(1, nt):
            total = total + sums[i, j]
        scale = lax.rsqrt(total * (1.0 / (nt * cols)) + 1e-06)
        column = jnp.concatenate(
            [jnp.transpose(jnp.broadcast_to(scale[:, j : j + 128], (128, 128))) for j in range(0, scale.shape[1], 128)],
            axis=0,
        )[0:rows]
        gain = gain_ref[:, pl.ds(pl.multiple_of(tp * cols, HEAD_DIM), cols)]
        wide = values.astype(jnp.float32) * gain
        parts = [wide[:, h * 128 : (h + 1) * 128] * column for h in range(heads)]
        return jnp.concatenate(parts, axis=1).astype(jnp.bfloat16)

    def kv_send(j):
        block = kvbuf.at[j, mine]
        send(block, block, xsend.at[3 + j], kvrecv.at[0, j], to_fore)
        send(block, block, xsend.at[3 + j], kvrecv.at[1, j], to_back)
        send(block, block, ssend.at[3 + j], kvsib.at[j], to_core)

    def kv_pass(j):
        block = kvbuf.at[j, of_back]
        arrived(block, kvrecv.at[0, j])
        send(block, block, xsend.at[3 + j], kvrecv.at[2, j], to_fore)
        send(block, block, ssend.at[3 + j], kvsib.at[j], to_core)

    def kv_far(j):
        for kind, piece in ((1, of_fore), (2, of_far)):
            block = kvbuf.at[j, piece]
            arrived(block, kvrecv.at[kind, j])
            send(block, block, ssend.at[3 + j], kvsib.at[j], to_core)

    send_own(0)
    send_rest(0)
    send_own(1)
    loads[1].wait()
    modulation[...] = table[steps_ref[0]]
    modulation[1:2, :] = modulation[1:2, :] + 1.0
    loads[0].wait()

    def early(i):
        norm_block(i)
        pl.when(i == 0)(lambda: send_own(2))
        pl.when(i == 1)(lambda: send_rest(1))
        pl.when(i == 3)(lambda: send_rest(2))

    slots(1, 1 + rows // norm_rows, early)
    for load in loads[2:]:
        load.wait()
    ends = [nz - 1 + SKEW * m + LAG_F for m in range(3)]
    done = 1 + rows // norm_rows
    rest_event(0)
    slots(done, ends[0] + 1)
    keys = project(0)
    send_sums(0, keys)
    kvbuf[0, mine] = keys
    rest_event(1)
    slots(ends[0] + 1, ends[1])
    kvbuf[0, mine] = normalise(0, kvbuf[0, mine], kgain_ref)
    kv_send(0)
    rest_event(2)
    slots(ends[1], ends[1] + 1)
    kvbuf[1, mine] = project(1)
    kv_send(1)
    kv_pass(0)
    slots(ends[1] + 1, ends[2] + 1)
    kv_far(0)
    kv_pass(1)
    kv_far(1)
    query = project(2)
    send_sums(1, query)
    arrived(kvbuf.at[0, pl.ds(0, nx)], kvsib.at[0])
    arrived(kvbuf.at[1, pl.ds(0, nx)], kvsib.at[1])
    qbuf[...] = normalise(1, query, qgain_ref)

    inverse_root = 1.0 / HEAD_DIM**0.5
    for h in range(heads):
        at = slice(h * HEAD_DIM, (h + 1) * HEAD_DIM)
        kh = kvbuf[0, :, :, at].reshape(2 * nx * rows, HEAD_DIM)
        vh = kvbuf[1, :, :, at].reshape(2 * nx * rows, HEAD_DIM)
        scores = dot(qbuf[:, at], kh, ((1,), (1,))) * inverse_root
        weights = jnp.exp(scores - jnp.max(scores, axis=-1, keepdims=True))
        total = jnp.sum(weights, axis=-1, keepdims=True)
        out_ref[:, at] = (dot(weights.astype(jnp.bfloat16), vh) / total).astype(jnp.bfloat16)


    def pieces(m, count):
        outer = max(a for a in range(1, nz + 1) if count % a == 0 and count // a <= 2 * nx)
        return wbuf.at[m, pl.ds(0, outer), pl.ds(0, count // outer)]

    def wait_sends(z_count, x_count):
        for m in range(3):
            sent(pieces(m, z_count), zsend.at[m])
            sent(pieces(m, x_count), xsend.at[m])

    pl.when(inside)(lambda: wait_sends(2 * nx + nz - 1, 3 * (nz - 3)))
    pl.when(jnp.logical_not(inside))(lambda: wait_sends(nx, 3 * (nz - 2)))
    for m in range(3):
        sent(wbuf.at[m, pl.ds(0, nz - 1), pl.ds(0, nx)], ssend.at[m])
    for j in range(2):
        sent(kvbuf.at[j, pl.ds(0, 3)], xsend.at[3 + j])
        sent(kvbuf.at[j, pl.ds(0, nx)], ssend.at[3 + j])
        sent(sums.at[j, pl.ds(0, nt - 1)], sumsend.at[j])


def local(sizes, latents, timesteps, mod_table, w_query, w_key, w_value, q_gain, k_gain):
    nz, nx, nt = sizes
    rows, width = latents.shape[2:]
    cols = w_query.shape[1]
    part = w_query.shape[0] // (2 * nx)
    hbm, vmem = pl.BlockSpec(memory_space=pl.ANY), pl.BlockSpec(memory_space=pltpu.VMEM)
    split = [w.reshape(2 * nx, part, cols) for w in (w_key, w_value, w_query)]
    dma = pltpu.SemaphoreType.DMA
    out = pl.pallas_call(
        functools.partial(kernel, sizes),
        out_shape=jax.ShapeDtypeStruct((rows, cols), jnp.bfloat16),
        in_specs=[pl.BlockSpec(memory_space=pltpu.SMEM), hbm, hbm, hbm, hbm, hbm, vmem, vmem],
        out_specs=vmem,
        scratch_shapes=[
            pltpu.VMEM((3, nz, 2 * nx, part, cols), jnp.bfloat16),
            pltpu.VMEM((rows, width), jnp.bfloat16),
            pltpu.VMEM(mod_table.shape, jnp.float32),
            pltpu.VMEM((2, width), jnp.float32),
            pltpu.VMEM((rows, width), jnp.bfloat16),
            pltpu.VMEM((rows, cols), jnp.float32),
            pltpu.VMEM((2, 2 * nx, rows, cols), jnp.bfloat16),
            pltpu.VMEM((rows, cols), jnp.bfloat16),
            pltpu.VMEM((2, nt, 1, (rows + 127) // 128 * 128), jnp.float32),
            dma((5,)),
            dma((3, nz)),
            dma((3, 2)),
            dma((3, 3, nz)),
            dma((3,)),
            dma((3, 2)),
            dma((2,)),
            dma((2,)),
            dma((3,)),
            dma((5,)),
            dma((5,)),
            dma((2,)),
        ],
        compiler_params=pltpu.CompilerParams(
            collective_id=0, has_side_effects=True, vmem_limit_bytes=48 * 1024 * 1024
        ),
    )(
        timesteps,
        latents.reshape(rows, width),
        mod_table,
        *split,
        k_gain.reshape(1, -1),
        q_gain.reshape(1, -1),
    )
    return out.reshape(1, 1, rows, cols)


def solution(mesh):
    sizes = (mesh.shape["rep"], mesh.shape["sp"] // 2, mesh.shape["tp"])
    return jax.shard_map(
        functools.partial(local, sizes),
        mesh=mesh,
        in_specs=(
            P("rep", None, "sp", None),
            P("rep"),
            P(),
            P("rep", "tp"),
            P("rep", "tp"),
            P("rep", "tp"),
            P(),
            P(),
        ),
        out_specs=P("rep", None, "sp", "tp"),
        check_vma=False,
    )
```

time: 238 us -> 117 us (0.49)
  waiting for transfers between devices: 162 us -> 0 us
  Pallas kernels: 0 us -> 106 us
  blocking collectives: 37.8 us -> 0 us
  between operations: 14.1 us -> 0.67 us
  matrix products: 8.57 us -> 0 us
  other arithmetic: 5.86 us -> 0 us
    all_gather x2 -> x0, waiting for transfers between devices: 162 us -> none  [the longest x1 134 us: local(): weights = lax.all_gather(stacked, ('rep', 'sp'), axis=0, tiled=True)]
    pallas_call x0 -> x1, Pallas kernels: none -> 106 us  [local(): pl.pallas_call(functools.partial(kernel, sizes), out_shape=jax.ShapeDtype...]
    psum x1 -> x0, blocking collectives: 37.8 us -> none  [local(): square = lax.psum(jnp.sum(pair * pair, axis=-1), 'tp') / inner]
    dot_general x3 -> x0, matrix products: 8.57 us -> none  [the longest x1 7.12 us: local(): jnp.dot(normed, weights, preferred_element_type=jnp.float32)]
    unnamed x4 -> x15, local copies, waits for them, and re-layouts: 1.03 us -> 8.28 us
    slice x4 -> x0, local copies, waits for them, and re-layouts: 5.12 us -> none  [the longest x2 3.51 us: local(): kh = both[0].reshape(-1, heads, HEAD_DIM)]
    reduce_sum x4 -> x0, other arithmetic: 3.36 us -> none  [the longest x1 1.9 us: local(): center = values - jnp.mean(values, axis=-1, keepdims=True)]
    dynamic_slice x4 -> x0, local copies, waits for them, and re-layouts: 2.42 us -> none  [the longest x2 1.55 us: local(): lax.dynamic_slice_in_dim(g, start, cols, 0)]
  transfers between devices with their start and end apart: 2 -> 0, of which waited for: 2 -> 0; matrix products, arithmetic and copies ran while one was open for 2% -> 0% of each run, Pallas kernels for 0% -> 0%
where the time goes in v2:
time: 117 us; the launch traced here: 115 us
  Pallas kernels  106 us (91%)
  local copies, waits for them, and re-layouts  8.28 us (7%)
    pallas_call x1, Pallas kernels, local(): pl.pallas_call(functools.partial(kernel, sizes), out_shape=jax.ShapeDtype...  106 us
    unnamed x15, local copies, waits for them, and re-layouts  8.28 us

profile of v2, /device:TPU:1, one launch (start us, length us, event | category | flops | bytes accessed | tf_op | source)
XLA Modules:
  0.0 115.3 jit_solution(13531638944215780166)
XLA Ops:
  0.7 0.0 copy-start
  0.7 1.6 %copy-done = f32[50,2,5120]{2,1,0:T(2,128)S(1)} copy-done((f32[50,2,5120]{2,1,0:T(2,128)S(1)}, f32[50,2,5120]{2,1,0:T(2,128)}, u32[]{:S(2)}) %copy-start) | copy-done | bytes 2048024
  2.2 0.0 copy-start.1
  2.2 1.5 %copy-done.1 = bf16[1,1,192,5120]{3,2,1,0:T(8,128)(2,1)S(1)} copy-done((bf16[1,1,192,5120]{3,2,1,0:T(8,128)(2,1)S(1)}, bf16[1,1,192,5120]{3,2,1,0:T(8,128)(2,1)}, u32[]{:S(2)}) %copy-start.1) | copy-done | bytes 1966104
  3.8 0.0 copy-start.2
  3.8 1.0 copy-done.2
  4.8 0.0 copy-start.3
  4.8 1.0 copy-done.3
  5.8 0.0 copy-start.4
  5.8 1.0 copy-done.4
  6.9 0.0 copy-start.5
  6.9 0.7 copy-done.5
  7.6 0.0 copy-start.6
  7.6 0.7 copy-done.6
  8.3 106.3 %shard_map.82 = bf16[192,384]{1,0:T(8,128)(2,1)S(1)} custom-call(s32[1]{0:T(128)S(6)} %copy.10.steps_ref, bf16[192,5120]{1,0:T(8,128)(2,1)S(1)} %bitcast.7, f32[50,2,5120]{2,1,0:T(2,128)S(1)} %copy-done, bf16[8,80,384]{2,1,0:T(8,128)(2,1)S(1)} %bitcast.9, bf16[8,80,384]{2,1,0:T(8,128)(2,1)S(1)} %bitcast.10, bf16[8,80,384]{2,1,0:T(8,128)(2,1)S(1)} %bitcast.11, ...), custom_call_target="tpu_custom_call" | custom-call | tf_op jit(solution)/shard_map/pallas_call | solution.py:287
  114.6 0.7 copy.11
Async XLA Ops:
  0.7 1.6 %copy-start = (f32[50,2,5120]{2,1,0:T(2,128)S(1)}, f32[50,2,5120]{2,1,0:T(2,128)}, u32[]{:S(2)}) copy-start(f32[50,2,5120]{2,1,0:T(2,128)} %table_hbm.1) | copy-start | bytes 6144004
  2.2 1.5 %copy-start.1 = (bf16[1,1,192,5120]{3,2,1,0:T(8,128)(2,1)S(1)}, bf16[1,1,192,5120]{3,2,1,0:T(8,128)(2,1)}, u32[]{:S(2)}) copy-start(bf16[1,1,192,5120]{3,2,1,0:T(8,128)(2,1)} %param.8) | copy-start | bytes 5898244
  3.8 1.0 copy-start.2
  4.8 1.0 copy-start.3
  5.8 1.0 copy-start.4
  6.9 0.7 copy-start.5
  7.6 0.7 copy-start.6

commit v3 on v2

--- a/solution.py
+++ b/solution.py
@@ -11,6 +11,7 @@
 SKEW = 2
 LAG_X = 1
 LAG_F = 2
+LAG_G = 3
 MESH = pl.DeviceIdType.MESH
 
 
@@ -20,9 +21,9 @@
 
 def kernel(
     sizes,
-    steps_ref, latents_hbm, table_hbm, wk_hbm, wv_hbm, wq_hbm, kgain_ref, qgain_ref,
+    steps_ref, latents_hbm, table_hbm, wk_hbm, wq_hbm, wv_hbm, kgain_ref, qgain_ref,
     out_ref,
-    wbuf, latents, table, modulation, normed, acc, kvbuf, qbuf, sums,
+    wbuf, latents, table, modulation, normed, acc, kvbuf, qbuf, probs, sums, token,
     local_sem, zrecv, zrest, xrecv, srecv, kvrecv, kvsib, sumrecv, zsend, xsend, ssend, sumsend,
 ):
     nz, nx, nt = sizes
@@ -34,7 +35,7 @@
     mine, of_back, of_fore, of_far = base + x, base + back, base + fore, base + (x + 2) % nx
     to_fore, to_back, to_core = {"sp": fore * 2 + c}, {"sp": back * 2 + c}, {"sp": s + 1 - 2 * c}
     up, down = {"rep": r + 1}, {"rep": r - 1}
-    whbm = (wk_hbm, wv_hbm, wq_hbm)
+    whbm = (wk_hbm, wq_hbm, wv_hbm)
     rows, width = latents.shape
     cols = kvbuf.shape[3]
     heads = cols // HEAD_DIM
@@ -59,15 +60,30 @@
     def greet(where):
         pl.semaphore_signal(barrier, inc=1, device_id=where, device_id_type=MESH)
 
-    for where in (to_fore, to_back, to_core):
+    ny = nt // 2
+    place = (tp // ny) * nz + r
+
+    def on_ring(z):
+        z = (z + 2 * nz) % (2 * nz)
+        return {"rep": z % nz, "tp": (z // nz) * ny + tp % ny}
+
+    ring_up, ring_down = on_ring(place + 1), on_ring(place - 1)
+    for where in (to_fore, to_back, to_core, ring_up, ring_down):
         greet(where)
-    for i in range(1, nt):
-        greet({"tp": (tp + i) % nt})
-    pl.when(r < nz - 1)(lambda: greet(up))
-    pl.when(r > 0)(lambda: greet(down))
-    inside = jnp.logical_and(r > 0, r < nz - 1)
-    pl.when(inside)(lambda: pl.semaphore_wait(barrier, 4 + nt))
-    pl.when(jnp.logical_not(inside))(lambda: pl.semaphore_wait(barrier, 3 + nt))
+    for i in range(1, ny):
+        greet({"tp": (tp // ny) * ny + (tp + i) % ny})
+    pl.semaphore_wait(barrier, 4 + ny)
+
+    def pass_token():
+        pl.semaphore_signal(token, inc=1, device_id=ring_up, device_id_type=MESH)
+
+    def token_event(t):
+        @pl.when(t <= nz)
+        def _():
+            pl.semaphore_wait(token, 1)
+            pl.when(t < nz)(pass_token)
+
+    pass_token()
 
     def both_ways(action):
         pl.when(r < nz - 1)(lambda: action(up, 0))
@@ -111,7 +127,7 @@
 
     def to_sibling(m, src):
         block = wbuf.at[m, src, pl.ds(base, nx)]
-        send(block, block, ssend.at[m], srecv.at[m], to_core)
+        send(block, block, ssend.at[m], srecv.at[m, src], to_core)
 
     def f_event(k, m):
         def one(src, way):
@@ -125,6 +141,18 @@
             arrived(wbuf.at[m, src, pl.ds(0, nx - 1)], zrest.at[m, way])
             to_sibling(m, src)
         over_sources(1, 1, one)
+
+    def add_source(m, src):
+        depth = width // nz
+        at = pl.ds(pl.multiple_of(src * depth, HEAD_DIM), depth)
+        acc[m] += dot(normed[:, at], wbuf[m, src].reshape(depth, cols))
+
+    def use(m, src):
+        arrived(wbuf.at[m, src, pl.ds(base, nx)], srecv.at[m, src])
+        add_source(m, src)
+
+    def g_event(k, least):
+        over_sources(k, least, lambda src, way: use(2, src))
 
     def slot(t):
         for m in range(3):
@@ -133,6 +161,8 @@
             x_event(t - SKEW * m - LAG_X, m)
         for m in range(3):
             f_event(t - SKEW * m - LAG_F, m)
+        g_event(t - SKEW * 2 - LAG_G, 2)
+        token_event(t)
 
     def slots(first, end, extra=None):
         @pl.loop(first, end)
@@ -152,15 +182,10 @@
         normed[at, :] = scaled.astype(jnp.bfloat16)
 
     def project(m):
-        arrived(wbuf.at[m, pl.ds(0, nz - 1), pl.ds(0, nx)], srecv.at[m])
-        depth = width // nz
-        acc[...] = jnp.zeros_like(acc)
-
         @pl.loop(0, nz)
         def _(src):
-            at = pl.ds(pl.multiple_of(src * depth, HEAD_DIM), depth)
-            acc[...] += dot(normed[:, at], wbuf[m, src].reshape(depth, cols))
-        return acc[...].astype(jnp.bfloat16)
+            pl.when(src == r)(lambda: add_source(m, src))
+            pl.when(src != r)(lambda: use(m, src))
 
     def send_sums(i, values):
         wide = values.astype(jnp.float32)
@@ -206,6 +231,7 @@
     send_own(0)
     send_rest(0)
     send_own(1)
+    acc[...] = jnp.zeros_like(acc)
     loads[1].wait()
     modulation[...] = table[steps_ref[0]]
     modulation[1:2, :] = modulation[1:2, :] + 1.0
@@ -217,45 +243,55 @@
         pl.when(i == 1)(lambda: send_rest(1))
         pl.when(i == 3)(lambda: send_rest(2))
 
-    slots(1, 1 + rows // norm_rows, early)
+    done = 1 + rows // norm_rows
+    slots(1, done, early)
     for load in loads[2:]:
         load.wait()
-    ends = [nz - 1 + SKEW * m + LAG_F for m in range(3)]
-    done = 1 + rows // norm_rows
+    add_source(2, r)
+    ends = [nz + SKEW * m + LAG_F for m in range(2)]
+    last = nz + SKEW * 2 + LAG_G
     rest_event(0)
-    slots(done, ends[0] + 1)
-    keys = project(0)
-    send_sums(0, keys)
-    kvbuf[0, mine] = keys
+    slots(done, ends[0])
+    project(0)
+    kvbuf[0, mine] = acc[0].astype(jnp.bfloat16)
+    send_sums(0, kvbuf[0, mine])
     rest_event(1)
-    slots(ends[0] + 1, ends[1])
+    slots(ends[0], ends[1])
+    project(1)
+    qbuf[...] = acc[1].astype(jnp.bfloat16)
+    send_sums(1, qbuf[...])
+    rest_event(2)
+    slots(ends[1], last - 1)
+    g_event(1, 1)
     kvbuf[0, mine] = normalise(0, kvbuf[0, mine], kgain_ref)
     kv_send(0)
-    rest_event(2)
-    slots(ends[1], ends[1] + 1)
-    kvbuf[1, mine] = project(1)
+    slots(last - 1, last)
+    kvbuf[1, mine] = acc[2].astype(jnp.bfloat16)
     kv_send(1)
     kv_pass(0)
-    slots(ends[1] + 1, ends[2] + 1)
+    qbuf[...] = normalise(1, qbuf[...], qgain_ref)
     kv_far(0)
     kv_pass(1)
-    kv_far(1)
-    query = project(2)
-    send_sums(1, query)
     arrived(kvbuf.at[0, pl.ds(0, nx)], kvsib.at[0])
-    arrived(kvbuf.at[1, pl.ds(0, nx)], kvsib.at[1])
-    qbuf[...] = normalise(1, query, qgain_ref)
 
     inverse_root = 1.0 / HEAD_DIM**0.5
+    keys_all = 2 * nx * rows
+    totals = []
     for h in range(heads):
         at = slice(h * HEAD_DIM, (h + 1) * HEAD_DIM)
-        kh = kvbuf[0, :, :, at].reshape(2 * nx * rows, HEAD_DIM)
-        vh = kvbuf[1, :, :, at].reshape(2 * nx * rows, HEAD_DIM)
-        scores = dot(qbuf[:, at], kh, ((1,), (1,))) * inverse_root
+        scores = dot(qbuf[:, at], kvbuf[0, :, :, at].reshape(keys_all, HEAD_DIM), ((1,), (1,))) * inverse_root
         weights = jnp.exp(scores - jnp.max(scores, axis=-1, keepdims=True))
-        total = jnp.sum(weights, axis=-1, keepdims=True)
-        out_ref[:, at] = (dot(weights.astype(jnp.bfloat16), vh) / total).astype(jnp.bfloat16)
-
+        totals.append(jnp.sum(weights, axis=-1, keepdims=True))
+        probs[h] = weights.astype(jnp.bfloat16)
+        if h == 0:
+            kv_far(1)
+    arrived(kvbuf.at[1, pl.ds(0, nx)], kvsib.at[1])
+    for h in range(heads):
+        at = slice(h * HEAD_DIM, (h + 1) * HEAD_DIM)
+        context = dot(probs[h], kvbuf[1, :, :, at].reshape(keys_all, HEAD_DIM)) / totals[h]
+        out_ref[:, at] = context.astype(jnp.bfloat16)
+
+    inside = jnp.logical_and(r > 0, r < nz - 1)
 
     def pieces(m, count):
         outer = max(a for a in range(1, nz + 1) if count % a == 0 and count // a <= 2 * nx)
@@ -282,7 +318,7 @@
     cols = w_query.shape[1]
     part = w_query.shape[0] // (2 * nx)
     hbm, vmem = pl.BlockSpec(memory_space=pl.ANY), pl.BlockSpec(memory_space=pltpu.VMEM)
-    split = [w.reshape(2 * nx, part, cols) for w in (w_key, w_value, w_query)]
+    split = [w.reshape(2 * nx, part, cols) for w in (w_key, w_query, w_value)]
     dma = pltpu.SemaphoreType.DMA
     out = pl.pallas_call(
         functools.partial(kernel, sizes),
@@ -295,15 +331,17 @@
             pltpu.VMEM(mod_table.shape, jnp.float32),
             pltpu.VMEM((2, width), jnp.float32),
             pltpu.VMEM((rows, width), jnp.bfloat16),
-            pltpu.VMEM((rows, cols), jnp.float32),
+            pltpu.VMEM((3, rows, cols), jnp.float32),
             pltpu.VMEM((2, 2 * nx, rows, cols), jnp.bfloat16),
             pltpu.VMEM((rows, cols), jnp.bfloat16),
+            pltpu.VMEM((cols // HEAD_DIM, rows, 2 * nx * rows), jnp.bfloat16),
             pltpu.VMEM((2, nt, 1, (rows + 127) // 128 * 128), jnp.float32),
+            pltpu.SemaphoreType.REGULAR,
             dma((5,)),
             dma((3, nz)),
             dma((3, 2)),
             dma((3, 3, nz)),
-            dma((3,)),
+            dma((3, nz)),
             dma((3, 2)),
             dma((2,)),
             dma((2,)),
@@ -313,7 +351,7 @@
             dma((2,)),
         ],
         compiler_params=pltpu.CompilerParams(
-            collective_id=0, has_side_effects=True, vmem_limit_bytes=48 * 1024 * 1024
+            collective_id=0, has_side_effects=True, vmem_limit_bytes=62 * 1024 * 1024
         ),
     )(
         timesteps,

time: 117 us -> 93.2 us (0.80); the launches traced: 115 us -> 93 us
  Pallas kernels: 106 us -> 90.7 us
  local copies, waits for them, and re-layouts: 8.28 us -> 1.59 us
    pallas_call x1, Pallas kernels: 106 us -> 90.7 us  [local(): pl.pallas_call(functools.partial(kernel, sizes), out_shape=jax.ShapeDtype...]
    unnamed x15 -> x1, local copies, waits for them, and re-layouts: 8.28 us -> 1.59 us
where the time goes in v3:
time: 93.2 us; the launch traced here: 93 us
  Pallas kernels  90.7 us (97%)
  local copies, waits for them, and re-layouts  1.59 us (2%)
    pallas_call x1, Pallas kernels, local(): pl.pallas_call(functools.partial(kernel, sizes), out_shape=jax.ShapeDtype...  90.7 us

profile of v3, /device:TPU:1, one launch (start us, length us, event | category | flops | bytes accessed | tf_op | source)
XLA Modules:
  0.0 93.0 jit_solution(16000743005739794592)
XLA Ops:
  0.7 90.7 %shard_map.82 = bf16[192,384]{1,0:T(8,128)(2,1)} custom-call(s32[1]{0:T(128)S(6)} %copy.10.steps_ref, bf16[192,5120]{1,0:T(8,128)(2,1)} %bitcast.7, f32[50,2,5120]{2,1,0:T(2,128)} %table_hbm.1, bf16[8,80,384]{2,1,0:T(8,128)(2,1)} %bitcast.9, bf16[8,80,384]{2,1,0:T(8,128)(2,1)} %bitcast.10, bf16[8,80,384]{2,1,0:T(8,128)(2,1)} %bitcast.11, ...), custom_call_target="tpu_custom_call" | custom-call | tf_op jit(solution)/shard_map/pallas_call | solution.py:323
  91.4 1.6 %copy.11 = bf16[1,1,192,384]{3,2,1,0:T(8,128)(2,1)} copy(bf16[1,1,192,384]{3,2,1,0:T(8,128)(2,1)} %bitcast.8) | data formatting | bytes 294912

commit v4 on v3

--- a/solution.py
+++ b/solution.py
@@ -8,7 +8,9 @@
 from jax.sharding import PartitionSpec as P
 
 HEAD_DIM = 128
-SKEW = 2
+OFFSETS = (0, 1, 3)
+REST_1 = 3
+REST_2 = 9
 LAG_X = 1
 LAG_F = 2
 LAG_G = 3
@@ -23,8 +25,8 @@
     sizes,
     steps_ref, latents_hbm, table_hbm, wk_hbm, wq_hbm, wv_hbm, kgain_ref, qgain_ref,
     out_ref,
-    wbuf, latents, table, modulation, normed, acc, kvbuf, qbuf, probs, sums, token,
-    local_sem, zrecv, zrest, xrecv, srecv, kvrecv, kvsib, sumrecv, zsend, xsend, ssend, sumsend,
+    wbuf, latents, table, modulation, normed, acc, kvbuf, qbuf, probs, sums, scales, scale_row, token,
+    local_sem, zrecv, zrest, xrecv, srecv, kvrecv, kvsib, sumrecv, scalerecv, zsend, xsend, ssend, sumsend, scalesend,
 ):
     nz, nx, nt = sizes
     r, s, tp = lax.axis_index("rep"), lax.axis_index("sp"), lax.axis_index("tp")
@@ -156,12 +158,12 @@
 
     def slot(t):
         for m in range(3):
-            z_event(t - SKEW * m, m)
+            z_event(t - OFFSETS[m], m)
         for m in range(3):
-            x_event(t - SKEW * m - LAG_X, m)
+            x_event(t - OFFSETS[m] - LAG_X, m)
         for m in range(3):
-            f_event(t - SKEW * m - LAG_F, m)
-        g_event(t - SKEW * 2 - LAG_G, 2)
+            f_event(t - OFFSETS[m] - LAG_F, m)
+        g_event(t - OFFSETS[2] - LAG_G, 2)
         token_event(t)
 
     def slots(first, end, extra=None):
@@ -195,20 +197,35 @@
         for j in range(1, nt):
             send(sums.at[i, tp], sums.at[i, tp], sumsend.at[i], sumrecv.at[i], {"tp": (tp + j) % nt})
 
-    def normalise(i, values, gain_ref):
+    def inverse_rms(i):
         arrived(sums.at[i, pl.ds(0, nt - 1)], sumrecv.at[i])
         total = sums[i, 0]
         for j in range(1, nt):
             total = total + sums[i, j]
-        scale = lax.rsqrt(total * (1.0 / (nt * cols)) + 1e-06)
+        return lax.rsqrt(total * (1.0 / (nt * cols)) + 1e-06)
+
+    def gain_of(gain_ref):
+        return gain_ref[:, pl.ds(pl.multiple_of(tp * cols, HEAD_DIM), cols)]
+
+    def share_key_scale():
+        scales[mine] = inverse_rms(0)
+        for j in range(1, 2 * nx):
+            send(scales.at[mine], scales.at[mine], scalesend, scalerecv, {"sp": (s + j) % (2 * nx)})
+
+    def key_scale():
+        arrived(scales.at[pl.ds(0, 2 * nx - 1)], scalerecv)
+        for j in range(2 * nx):
+            scale_row[:, j * rows : (j + 1) * rows] = scales[j, :, 0:rows]
+
+    def normalise_query():
+        scale = inverse_rms(1)
         column = jnp.concatenate(
             [jnp.transpose(jnp.broadcast_to(scale[:, j : j + 128], (128, 128))) for j in range(0, scale.shape[1], 128)],
             axis=0,
         )[0:rows]
-        gain = gain_ref[:, pl.ds(pl.multiple_of(tp * cols, HEAD_DIM), cols)]
-        wide = values.astype(jnp.float32) * gain
+        wide = qbuf[...].astype(jnp.float32) * gain_of(qgain_ref)
         parts = [wide[:, h * 128 : (h + 1) * 128] * column for h in range(heads)]
-        return jnp.concatenate(parts, axis=1).astype(jnp.bfloat16)
+        qbuf[...] = jnp.concatenate(parts, axis=1).astype(jnp.bfloat16)
 
     def kv_send(j):
         block = kvbuf.at[j, mine]
@@ -229,8 +246,8 @@
             send(block, block, ssend.at[3 + j], kvsib.at[j], to_core)
 
     send_own(0)
+    send_own(1)
     send_rest(0)
-    send_own(1)
     acc[...] = jnp.zeros_like(acc)
     loads[1].wait()
     modulation[...] = table[steps_ref[0]]
@@ -239,38 +256,41 @@
 
     def early(i):
         norm_block(i)
-        pl.when(i == 0)(lambda: send_own(2))
-        pl.when(i == 1)(lambda: send_rest(1))
-        pl.when(i == 3)(lambda: send_rest(2))
+        pl.when(i == OFFSETS[2] - 1)(lambda: send_own(2))
+        pl.when(i == REST_1)(lambda: send_rest(1))
 
     done = 1 + rows // norm_rows
     slots(1, done, early)
     for load in loads[2:]:
         load.wait()
     add_source(2, r)
-    ends = [nz + SKEW * m + LAG_F for m in range(2)]
-    last = nz + SKEW * 2 + LAG_G
+    ends = [nz + at + LAG_F for at in OFFSETS]
     rest_event(0)
-    slots(done, ends[0])
+    slots(done, REST_2)
+    send_rest(2)
+    slots(REST_2, ends[0])
     project(0)
-    kvbuf[0, mine] = acc[0].astype(jnp.bfloat16)
-    send_sums(0, kvbuf[0, mine])
+    keys = acc[0].astype(jnp.bfloat16)
+    kvbuf[0, mine] = (keys.astype(jnp.float32) * gain_of(kgain_ref)).astype(jnp.bfloat16)
+    kv_send(0)
+    send_sums(0, keys)
     rest_event(1)
     slots(ends[0], ends[1])
     project(1)
     qbuf[...] = acc[1].astype(jnp.bfloat16)
     send_sums(1, qbuf[...])
+    kv_pass(0)
     rest_event(2)
-    slots(ends[1], last - 1)
+    slots(ends[1], ends[2] - 1)
+    kv_far(0)
     g_event(1, 1)
-    kvbuf[0, mine] = normalise(0, kvbuf[0, mine], kgain_ref)
-    kv_send(0)
-    slots(last - 1, last)
+    slots(ends[2] - 1, ends[2])
+    share_key_scale()
+    slots(ends[2], nz + OFFSETS[2] + LAG_G)
     kvbuf[1, mine] = acc[2].astype(jnp.bfloat16)
     kv_send(1)
-    kv_pass(0)
-    qbuf[...] = normalise(1, qbuf[...], qgain_ref)
-    kv_far(0)
+    normalise_query()
+    key_scale()
     kv_pass(1)
     arrived(kvbuf.at[0, pl.ds(0, nx)], kvsib.at[0])
 
@@ -279,7 +299,7 @@
     totals = []
     for h in range(heads):
         at = slice(h * HEAD_DIM, (h + 1) * HEAD_DIM)
-        scores = dot(qbuf[:, at], kvbuf[0, :, :, at].reshape(keys_all, HEAD_DIM), ((1,), (1,))) * inverse_root
+        scores = dot(qbuf[:, at], kvbuf[0, :, :, at].reshape(keys_all, HEAD_DIM), ((1,), (1,))) * (scale_row[...] * inverse_root)
         weights = jnp.exp(scores - jnp.max(scores, axis=-1, keepdims=True))
         totals.append(jnp.sum(weights, axis=-1, keepdims=True))
         probs[h] = weights.astype(jnp.bfloat16)
@@ -310,6 +330,7 @@
         sent(kvbuf.at[j, pl.ds(0, 3)], xsend.at[3 + j])
         sent(kvbuf.at[j, pl.ds(0, nx)], ssend.at[3 + j])
         sent(sums.at[j, pl.ds(0, nt - 1)], sumsend.at[j])
+    sent(scales.at[pl.ds(0, 2 * nx - 1)], scalesend)
 
 
 def local(sizes, latents, timesteps, mod_table, w_query, w_key, w_value, q_gain, k_gain):
@@ -336,6 +357,8 @@
             pltpu.VMEM((rows, cols), jnp.bfloat16),
             pltpu.VMEM((cols // HEAD_DIM, rows, 2 * nx * rows), jnp.bfloat16),
             pltpu.VMEM((2, nt, 1, (rows + 127) // 128 * 128), jnp.float32),
+            pltpu.VMEM((2 * nx, 1, (rows + 127) // 128 * 128), jnp.float32),
+            pltpu.VMEM((1, 2 * nx * rows), jnp.float32),
             pltpu.SemaphoreType.REGULAR,
             dma((5,)),
             dma((3, nz)),
@@ -345,10 +368,12 @@
             dma((3, 2)),
             dma((2,)),
             dma((2,)),
+            dma,
             dma((3,)),
             dma((5,)),
             dma((5,)),
             dma((2,)),
+            dma,
         ],
         compiler_params=pltpu.CompilerParams(
             collective_id=0, has_side_effects=True, vmem_limit_bytes=62 * 1024 * 1024

time: 93.2 us -> 87.5 us (0.939)
  Pallas kernels: 90.7 us -> 85 us
    pallas_call x1, Pallas kernels: 90.7 us -> 85 us  [local(): pl.pallas_call(functools.partial(kernel, sizes), out_shape=jax.ShapeDtype...]
where the time goes in v4:
time: 87.5 us; the launch traced here: 87.3 us
  Pallas kernels  85 us (97%)
  local copies, waits for them, and re-layouts  1.59 us (2%)
    pallas_call x1, Pallas kernels, local(): pl.pallas_call(functools.partial(kernel, sizes), out_shape=jax.ShapeDtype...  85 us

profile of v4, /device:TPU:1, one launch (start us, length us, event | category | flops | bytes accessed | tf_op | source)
XLA Modules:
  0.0 87.3 jit_solution(14126215286102582331)
XLA Ops:
  0.7 85.0 %shard_map.82 = bf16[192,384]{1,0:T(8,128)(2,1)} custom-call(s32[1]{0:T(128)S(6)} %copy.10.steps_ref, bf16[192,5120]{1,0:T(8,128)(2,1)} %bitcast.7, f32[50,2,5120]{2,1,0:T(2,128)} %table_hbm.1, bf16[8,80,384]{2,1,0:T(8,128)(2,1)} %bitcast.9, bf16[8,80,384]{2,1,0:T(8,128)(2,1)} %bitcast.10, bf16[8,80,384]{2,1,0:T(8,128)(2,1)} %bitcast.11, ...), custom_call_target="tpu_custom_call" | custom-call | tf_op jit(solution)/shard_map/pallas_call | solution.py:344
  85.7 1.6 %copy.11 = bf16[1,1,192,384]{3,2,1,0:T(8,128)(2,1)} copy(bf16[1,1,192,384]{3,2,1,0:T(8,128)(2,1)} %bitcast.8) | data formatting | bytes 294912

commit v5 on v4

--- a/solution.py
+++ b/solution.py
@@ -9,8 +9,7 @@
 
 HEAD_DIM = 128
 OFFSETS = (0, 1, 3)
-REST_1 = 3
-REST_2 = 9
+PAIRS = (False, False, True)
 LAG_X = 1
 LAG_F = 2
 LAG_G = 3
@@ -25,8 +24,8 @@
     sizes,
     steps_ref, latents_hbm, table_hbm, wk_hbm, wq_hbm, wv_hbm, kgain_ref, qgain_ref,
     out_ref,
-    wbuf, latents, table, modulation, normed, acc, kvbuf, qbuf, probs, sums, scales, scale_row, token,
-    local_sem, zrecv, zrest, xrecv, srecv, kvrecv, kvsib, sumrecv, scalerecv, zsend, xsend, ssend, sumsend, scalesend,
+    wbuf, latents, table, modulation, normed, acc, kvbuf, qbuf, probs, sums, scales, knbuf, answered,
+    local_sem, zrecv, zfar, xrecv, srecv, kvrecv, kvsib, sumrecv, scalerecv, zsend, xsend, ssend, sumsend, scalesend,
 ):
     nz, nx, nt = sizes
     r, s, tp = lax.axis_index("rep"), lax.axis_index("sp"), lax.axis_index("tp")
@@ -63,42 +62,42 @@
         pl.semaphore_signal(barrier, inc=1, device_id=where, device_id_type=MESH)
 
     ny = nt // 2
-    place = (tp // ny) * nz + r
-
-    def on_ring(z):
-        z = (z + 2 * nz) % (2 * nz)
-        return {"rep": z % nz, "tp": (z // nz) * ny + tp % ny}
-
-    ring_up, ring_down = on_ring(place + 1), on_ring(place - 1)
-    for where in (to_fore, to_back, to_core, ring_up, ring_down):
+    lower = tp < ny
+
+    def far_peers(action):
+        for i in range(ny):
+            action({"tp": (tp + ny) % nt // ny * ny + i})
+
+    for where in (to_fore, to_back, to_core):
         greet(where)
+    pl.when(r < nz - 1)(lambda: greet(up))
+    pl.when(r > 0)(lambda: greet(down))
     for i in range(1, ny):
         greet({"tp": (tp // ny) * ny + (tp + i) % ny})
-    pl.semaphore_wait(barrier, 4 + ny)
-
-    def pass_token():
-        pl.semaphore_signal(token, inc=1, device_id=ring_up, device_id_type=MESH)
-
-    def token_event(t):
-        @pl.when(t <= nz)
-        def _():
-            pl.semaphore_wait(token, 1)
-            pl.when(t < nz)(pass_token)
-
-    pass_token()
+    pl.when(lower)(lambda: far_peers(greet))
+    at_end = jnp.logical_or(r == 0, r == nz - 1)
+
+    def wait_greetings(near):
+        pl.when(lower)(lambda: pl.semaphore_wait(barrier, near))
+        pl.when(jnp.logical_not(lower))(lambda: pl.semaphore_wait(barrier, near + ny))
+
+    pl.when(at_end)(lambda: wait_greetings(3 + ny))
+    pl.when(jnp.logical_not(at_end))(lambda: wait_greetings(4 + ny))
+
+    def answer(where):
+        pl.semaphore_signal(answered, inc=1, device_id=where, device_id_type=MESH)
+
+    pl.when(jnp.logical_not(lower))(lambda: far_peers(answer))
 
     def both_ways(action):
         pl.when(r < nz - 1)(lambda: action(up, 0))
         pl.when(r > 0)(lambda: action(down, 1))
 
     def send_own(m):
-        both_ways(lambda where, way: send(whbm[m].at[mine], wbuf.at[m, r, mine], zsend.at[m], zrecv.at[m, r], where))
-
-    def send_rest(m):
         def one(where, way):
-            for i in range(1, nx):
-                piece = base + (x + i) % nx
-                send(whbm[m].at[piece], wbuf.at[m, r, piece], zsend.at[m], zrest.at[m, way], where)
+            send(whbm[m].at[mine], wbuf.at[m, r, mine], zsend.at[m], zrecv.at[m, r], where)
+            if PAIRS[m]:
+                send(whbm[m].at[of_far], wbuf.at[m, r, of_far], zsend.at[m], zfar.at[m, r], where)
         both_ways(one)
 
     def over_sources(k, least, action):
@@ -107,42 +106,55 @@
 
     def z_event(k, m):
         def one(src, way):
+            def pass_on(place, sems):
+                piece = wbuf.at[m, src, place]
+                arrived(piece, sems.at[m, src])
+                if way == 0:
+                    pl.when(r < nz - 1)(lambda: send(piece, piece, zsend.at[m], sems.at[m, src], up))
+                else:
+                    pl.when(r > 0)(lambda: send(piece, piece, zsend.at[m], sems.at[m, src], down))
+
+            pass_on(mine, zrecv)
             piece = wbuf.at[m, src, mine]
-            arrived(piece, zrecv.at[m, src])
-            if way == 0:
-                pl.when(r < nz - 1)(lambda: send(piece, piece, zsend.at[m], zrecv.at[m, src], up))
-            else:
-                pl.when(r > 0)(lambda: send(piece, piece, zsend.at[m], zrecv.at[m, src], down))
-
-            @pl.when(k >= 2)
-            def _():
-                send(piece, piece, xsend.at[m], xrecv.at[0, m, src], to_fore)
-                send(piece, piece, xsend.at[m], xrecv.at[1, m, src], to_back)
+            send(piece, piece, xsend.at[m], xrecv.at[0, m, src], to_fore)
+            send(piece, piece, xsend.at[m], xrecv.at[1, m, src], to_back)
+            if PAIRS[m]:
+                pass_on(of_far, zfar)
         over_sources(k, 1, one)
 
-    def x_event(k, m):
-        def one(src, way):
+    upper = r // (nz // 2)
+    edge = r + upper * (nz - 1 - 2 * r)
+
+    def nth_source(n, action):
+        @pl.when(jnp.logical_and(n >= 1, n <= nz - 1))
+        def _():
+            both = n <= 2 * edge
+            sign = jnp.where(both, 2 * ((n - 1) % 2) - 1, 1 - 2 * upper)
+            action(r + sign * jnp.where(both, (n + 1) // 2, n - edge))
+
+    def x_event(n, m):
+        if PAIRS[m]:
+            return
+
+        def one(src):
             piece = wbuf.at[m, src, of_back]
             arrived(piece, xrecv.at[0, m, src])
             send(piece, piece, xsend.at[m], xrecv.at[2, m, src], to_fore)
-        over_sources(k, 2, one)
+        nth_source(n, one)
 
     def to_sibling(m, src):
         block = wbuf.at[m, src, pl.ds(base, nx)]
         send(block, block, ssend.at[m], srecv.at[m, src], to_core)
 
-    def f_event(k, m):
-        def one(src, way):
+    def f_event(n, m):
+        def one(src):
             arrived(wbuf.at[m, src, of_fore], xrecv.at[1, m, src])
-            arrived(wbuf.at[m, src, of_far], xrecv.at[2, m, src])
+            if PAIRS[m]:
+                arrived(wbuf.at[m, src, of_back], xrecv.at[0, m, src])
+            else:
+                arrived(wbuf.at[m, src, of_far], xrecv.at[2, m, src])
             to_sibling(m, src)
-        over_sources(k, 2, one)
-
-    def rest_event(m):
-        def one(src, way):
-            arrived(wbuf.at[m, src, pl.ds(0, nx - 1)], zrest.at[m, way])
-            to_sibling(m, src)
-        over_sources(1, 1, one)
+        nth_source(n, one)
 
     def add_source(m, src):
         depth = width // nz
@@ -153,8 +165,8 @@
         arrived(wbuf.at[m, src, pl.ds(base, nx)], srecv.at[m, src])
         add_source(m, src)
 
-    def g_event(k, least):
-        over_sources(k, least, lambda src, way: use(2, src))
+    def g_event(n):
+        nth_source(n, lambda src: use(2, src))
 
     def slot(t):
         for m in range(3):
@@ -163,8 +175,7 @@
             x_event(t - OFFSETS[m] - LAG_X, m)
         for m in range(3):
             f_event(t - OFFSETS[m] - LAG_F, m)
-        g_event(t - OFFSETS[2] - LAG_G, 2)
-        token_event(t)
+        g_event(t - OFFSETS[2] - LAG_G)
 
     def slots(first, end, extra=None):
         @pl.loop(first, end)
@@ -212,31 +223,35 @@
         for j in range(1, 2 * nx):
             send(scales.at[mine], scales.at[mine], scalesend, scalerecv, {"sp": (s + j) % (2 * nx)})
 
-    def key_scale():
-        arrived(scales.at[pl.ds(0, 2 * nx - 1)], scalerecv)
-        for j in range(2 * nx):
-            scale_row[:, j * rows : (j + 1) * rows] = scales[j, :, 0:rows]
-
-    def normalise_query():
-        scale = inverse_rms(1)
+    def normalise(values, scale, gain_ref):
         column = jnp.concatenate(
             [jnp.transpose(jnp.broadcast_to(scale[:, j : j + 128], (128, 128))) for j in range(0, scale.shape[1], 128)],
             axis=0,
         )[0:rows]
-        wide = qbuf[...].astype(jnp.float32) * gain_of(qgain_ref)
+        wide = values.astype(jnp.float32) * gain_of(gain_ref)
         parts = [wide[:, h * 128 : (h + 1) * 128] * column for h in range(heads)]
-        qbuf[...] = jnp.concatenate(parts, axis=1).astype(jnp.bfloat16)
+        return jnp.concatenate(parts, axis=1).astype(jnp.bfloat16)
+
+    def normalise_keys():
+        arrived(scales.at[pl.ds(0, 2 * nx - 1)], scalerecv)
+
+        @pl.loop(0, 2 * nx)
+        def _(j):
+            knbuf[j] = normalise(kvbuf[0, j], scales[j], kgain_ref)
 
     def kv_send(j):
         block = kvbuf.at[j, mine]
         send(block, block, xsend.at[3 + j], kvrecv.at[0, j], to_fore)
         send(block, block, xsend.at[3 + j], kvrecv.at[1, j], to_back)
         send(block, block, ssend.at[3 + j], kvsib.at[j], to_core)
+        if j == 1:
+            send(block, block, xsend.at[3 + j], kvrecv.at[2, j], {"sp": (x + 2) % nx * 2 + c})
 
     def kv_pass(j):
         block = kvbuf.at[j, of_back]
         arrived(block, kvrecv.at[0, j])
-        send(block, block, xsend.at[3 + j], kvrecv.at[2, j], to_fore)
+        if j == 0:
+            send(block, block, xsend.at[3 + j], kvrecv.at[2, j], to_fore)
         send(block, block, ssend.at[3 + j], kvsib.at[j], to_core)
 
     def kv_far(j):
@@ -247,7 +262,6 @@
 
     send_own(0)
     send_own(1)
-    send_rest(0)
     acc[...] = jnp.zeros_like(acc)
     loads[1].wait()
     modulation[...] = table[steps_ref[0]]
@@ -257,7 +271,6 @@
     def early(i):
         norm_block(i)
         pl.when(i == OFFSETS[2] - 1)(lambda: send_own(2))
-        pl.when(i == REST_1)(lambda: send_rest(1))
 
     done = 1 + rows // norm_rows
     slots(1, done, early)
@@ -265,45 +278,39 @@
         load.wait()
     add_source(2, r)
     ends = [nz + at + LAG_F for at in OFFSETS]
-    rest_event(0)
-    slots(done, REST_2)
-    send_rest(2)
-    slots(REST_2, ends[0])
+    slots(done, ends[0])
     project(0)
-    keys = acc[0].astype(jnp.bfloat16)
-    kvbuf[0, mine] = (keys.astype(jnp.float32) * gain_of(kgain_ref)).astype(jnp.bfloat16)
+    kvbuf[0, mine] = acc[0].astype(jnp.bfloat16)
     kv_send(0)
-    send_sums(0, keys)
-    rest_event(1)
+    pl.when(lower)(lambda: pl.semaphore_wait(answered, ny))
+    send_sums(0, kvbuf[0, mine])
     slots(ends[0], ends[1])
     project(1)
     qbuf[...] = acc[1].astype(jnp.bfloat16)
     send_sums(1, qbuf[...])
     kv_pass(0)
-    rest_event(2)
     slots(ends[1], ends[2] - 1)
     kv_far(0)
-    g_event(1, 1)
     slots(ends[2] - 1, ends[2])
     share_key_scale()
     slots(ends[2], nz + OFFSETS[2] + LAG_G)
     kvbuf[1, mine] = acc[2].astype(jnp.bfloat16)
     kv_send(1)
-    normalise_query()
-    key_scale()
-    kv_pass(1)
     arrived(kvbuf.at[0, pl.ds(0, nx)], kvsib.at[0])
+    normalise_keys()
+    qbuf[...] = normalise(qbuf[...], inverse_rms(1), qgain_ref)
 
     inverse_root = 1.0 / HEAD_DIM**0.5
     keys_all = 2 * nx * rows
     totals = []
     for h in range(heads):
         at = slice(h * HEAD_DIM, (h + 1) * HEAD_DIM)
-        scores = dot(qbuf[:, at], kvbuf[0, :, :, at].reshape(keys_all, HEAD_DIM), ((1,), (1,))) * (scale_row[...] * inverse_root)
+        scores = dot(qbuf[:, at], knbuf[:, :, at].reshape(keys_all, HEAD_DIM), ((1,), (1,))) * inverse_root
         weights = jnp.exp(scores - jnp.max(scores, axis=-1, keepdims=True))
         totals.append(jnp.sum(weights, axis=-1, keepdims=True))
         probs[h] = weights.astype(jnp.bfloat16)
         if h == 0:
+            kv_pass(1)
             kv_far(1)
     arrived(kvbuf.at[1, pl.ds(0, nx)], kvsib.at[1])
     for h in range(heads):
@@ -311,19 +318,19 @@
         context = dot(probs[h], kvbuf[1, :, :, at].reshape(keys_all, HEAD_DIM)) / totals[h]
         out_ref[:, at] = context.astype(jnp.bfloat16)
 
-    inside = jnp.logical_and(r > 0, r < nz - 1)
 
     def pieces(m, count):
         outer = max(a for a in range(1, nz + 1) if count % a == 0 and count // a <= 2 * nx)
         return wbuf.at[m, pl.ds(0, outer), pl.ds(0, count // outer)]
 
-    def wait_sends(z_count, x_count):
+    def wait_sends(count):
         for m in range(3):
-            sent(pieces(m, z_count), zsend.at[m])
-            sent(pieces(m, x_count), xsend.at[m])
-
-    pl.when(inside)(lambda: wait_sends(2 * nx + nz - 1, 3 * (nz - 3)))
-    pl.when(jnp.logical_not(inside))(lambda: wait_sends(nx, 3 * (nz - 2)))
+            sent(pieces(m, count * (2 if PAIRS[m] else 1)), zsend.at[m])
+
+    pl.when(edge > 0)(lambda: wait_sends(nz + 1))
+    pl.when(edge == 0)(lambda: wait_sends(1))
+    for m in range(3):
+        sent(pieces(m, (nz - 1) * (2 if PAIRS[m] else 3)), xsend.at[m])
     for m in range(3):
         sent(wbuf.at[m, pl.ds(0, nz - 1), pl.ds(0, nx)], ssend.at[m])
     for j in range(2):
@@ -358,14 +365,14 @@
             pltpu.VMEM((cols // HEAD_DIM, rows, 2 * nx * rows), jnp.bfloat16),
             pltpu.VMEM((2, nt, 1, (rows + 127) // 128 * 128), jnp.float32),
             pltpu.VMEM((2 * nx, 1, (rows + 127) // 128 * 128), jnp.float32),
-            pltpu.VMEM((1, 2 * nx * rows), jnp.float32),
+            pltpu.VMEM((2 * nx, rows, cols), jnp.bfloat16),
             pltpu.SemaphoreType.REGULAR,
             dma((5,)),
             dma((3, nz)),
-            dma((3, 2)),
+            dma((3, nz)),
             dma((3, 3, nz)),
             dma((3, nz)),
-            dma((3, 2)),
+            dma((3, nz)),
             dma((2,)),
             dma((2,)),
             dma,

time: 87.5 us -> 84.1 us (0.961)
  Pallas kernels: 85 us -> 81.6 us
    pallas_call x1, Pallas kernels: 85 us -> 81.6 us  [local(): pl.pallas_call(functools.partial(kernel, sizes), out_shape=jax.ShapeDtype...]
where the time goes in v5:
time: 84.1 us; the launch traced here: 83.8 us
  Pallas kernels  81.6 us (97%)
  local copies, waits for them, and re-layouts  1.59 us (2%)
    pallas_call x1, Pallas kernels, local(): pl.pallas_call(functools.partial(kernel, sizes), out_shape=jax.ShapeDtype...  81.6 us

profile of v5, /device:TPU:1, one launch (start us, length us, event | category | flops | bytes accessed | tf_op | source)
XLA Modules:
  0.0 83.8 jit_solution(4967272343277777591)
XLA Ops:
  0.7 81.6 %shard_map.82 = bf16[192,384]{1,0:T(8,128)(2,1)} custom-call(s32[1]{0:T(128)S(6)} %copy.10.steps_ref, bf16[192,5120]{1,0:T(8,128)(2,1)} %bitcast.7, f32[50,2,5120]{2,1,0:T(2,128)} %table_hbm.1, bf16[8,80,384]{2,1,0:T(8,128)(2,1)} %bitcast.9, bf16[8,80,384]{2,1,0:T(8,128)(2,1)} %bitcast.10, bf16[8,80,384]{2,1,0:T(8,128)(2,1)} %bitcast.11, ...), custom_call_target="tpu_custom_call" | custom-call | tf_op jit(solution)/shard_map/pallas_call | solution.py:351
  82.2 1.6 %copy.11 = bf16[1,1,192,384]{3,2,1,0:T(8,128)(2,1)} copy(bf16[1,1,192,384]{3,2,1,0:T(8,128)(2,1)} %bitcast.8) | data formatting | bytes 294912

commit v6 on v5

--- a/solution.py
+++ b/solution.py
@@ -8,8 +8,8 @@
 from jax.sharding import PartitionSpec as P
 
 HEAD_DIM = 128
-OFFSETS = (0, 1, 3)
-PAIRS = (False, False, True)
+OFFSETS = (0, 1, 2, 3)
+PAIRS = (False, False, True, True)
 LAG_X = 1
 LAG_F = 2
 LAG_G = 3
@@ -41,6 +41,24 @@
     cols = kvbuf.shape[3]
     heads = cols // HEAD_DIM
 
+    split = cols - HEAD_DIM
+    streams = ((0, 0, cols), (1, 0, cols), (2, 0, split), (2, split, cols))
+    count = len(streams)
+
+    def weight(m, src, piece):
+        which, first, end = streams[m]
+        return wbuf.at[which, src, piece, :, pl.ds(first, end - first)]
+
+    def own_weight(m, piece):
+        which, first, end = streams[m]
+        return whbm[which].at[piece, :, pl.ds(first, end - first)]
+
+    shared = ((0, 0, cols), (1, 0, split), (1, split, cols))
+
+    def kv_part(j, piece):
+        which, first, end = shared[j]
+        return kvbuf.at[which, piece, :, pl.ds(first, end - first)]
+
     def send(src, dst, send_sem, recv_sem, where):
         pltpu.make_async_remote_copy(src, dst, send_sem, recv_sem, device_id=where, device_id_type=MESH).start()
 
@@ -95,9 +113,9 @@
 
     def send_own(m):
         def one(where, way):
-            send(whbm[m].at[mine], wbuf.at[m, r, mine], zsend.at[m], zrecv.at[m, r], where)
+            send(own_weight(m, mine), weight(m, r, mine), zsend.at[m], zrecv.at[m, r], where)
             if PAIRS[m]:
-                send(whbm[m].at[of_far], wbuf.at[m, r, of_far], zsend.at[m], zfar.at[m, r], where)
+                send(own_weight(m, of_far), weight(m, r, of_far), zsend.at[m], zfar.at[m, r], where)
         both_ways(one)
 
     def over_sources(k, least, action):
@@ -107,7 +125,7 @@
     def z_event(k, m):
         def one(src, way):
             def pass_on(place, sems):
-                piece = wbuf.at[m, src, place]
+                piece = weight(m, src, place)
                 arrived(piece, sems.at[m, src])
                 if way == 0:
                     pl.when(r < nz - 1)(lambda: send(piece, piece, zsend.at[m], sems.at[m, src], up))
@@ -115,7 +133,7 @@
                     pl.when(r > 0)(lambda: send(piece, piece, zsend.at[m], sems.at[m, src], down))
 
             pass_on(mine, zrecv)
-            piece = wbuf.at[m, src, mine]
+            piece = weight(m, src, mine)
             send(piece, piece, xsend.at[m], xrecv.at[0, m, src], to_fore)
             send(piece, piece, xsend.at[m], xrecv.at[1, m, src], to_back)
             if PAIRS[m]:
@@ -137,45 +155,47 @@
             return
 
         def one(src):
-            piece = wbuf.at[m, src, of_back]
+            piece = weight(m, src, of_back)
             arrived(piece, xrecv.at[0, m, src])
             send(piece, piece, xsend.at[m], xrecv.at[2, m, src], to_fore)
         nth_source(n, one)
 
     def to_sibling(m, src):
-        block = wbuf.at[m, src, pl.ds(base, nx)]
+        block = weight(m, src, pl.ds(base, nx))
         send(block, block, ssend.at[m], srecv.at[m, src], to_core)
 
     def f_event(n, m):
         def one(src):
-            arrived(wbuf.at[m, src, of_fore], xrecv.at[1, m, src])
+            arrived(weight(m, src, of_fore), xrecv.at[1, m, src])
             if PAIRS[m]:
-                arrived(wbuf.at[m, src, of_back], xrecv.at[0, m, src])
+                arrived(weight(m, src, of_back), xrecv.at[0, m, src])
             else:
-                arrived(wbuf.at[m, src, of_far], xrecv.at[2, m, src])
+                arrived(weight(m, src, of_far), xrecv.at[2, m, src])
             to_sibling(m, src)
         nth_source(n, one)
 
     def add_source(m, src):
         depth = width // nz
         at = pl.ds(pl.multiple_of(src * depth, HEAD_DIM), depth)
-        acc[m] += dot(normed[:, at], wbuf[m, src].reshape(depth, cols))
+        which, first, end = streams[m]
+        acc[which, :, first:end] += dot(normed[:, at], wbuf[which, src, :, :, first:end].reshape(depth, end - first))
 
     def use(m, src):
-        arrived(wbuf.at[m, src, pl.ds(base, nx)], srecv.at[m, src])
+        arrived(weight(m, src, pl.ds(base, nx)), srecv.at[m, src])
         add_source(m, src)
 
-    def g_event(n):
-        nth_source(n, lambda src: use(2, src))
+    def g_event(n, m):
+        nth_source(n, lambda src: use(m, src))
 
     def slot(t):
-        for m in range(3):
+        for m in range(count):
             z_event(t - OFFSETS[m], m)
-        for m in range(3):
+        for m in range(count):
             x_event(t - OFFSETS[m] - LAG_X, m)
-        for m in range(3):
+        for m in range(count):
             f_event(t - OFFSETS[m] - LAG_F, m)
-        g_event(t - OFFSETS[2] - LAG_G)
+        for m in range(2, count):
+            g_event(t - OFFSETS[m] - LAG_G, m)
 
     def slots(first, end, extra=None):
         @pl.loop(first, end)
@@ -184,7 +204,7 @@
             if extra is not None:
                 extra(t - first)
 
-    norm_rows = rows // 6 if rows % 96 == 0 else rows // 2
+    norm_rows = rows // 4
 
     def norm_block(i):
         at = pl.ds(pl.multiple_of(i * norm_rows, norm_rows), norm_rows)
@@ -240,25 +260,25 @@
             knbuf[j] = normalise(kvbuf[0, j], scales[j], kgain_ref)
 
     def kv_send(j):
-        block = kvbuf.at[j, mine]
-        send(block, block, xsend.at[3 + j], kvrecv.at[0, j], to_fore)
-        send(block, block, xsend.at[3 + j], kvrecv.at[1, j], to_back)
-        send(block, block, ssend.at[3 + j], kvsib.at[j], to_core)
-        if j == 1:
-            send(block, block, xsend.at[3 + j], kvrecv.at[2, j], {"sp": (x + 2) % nx * 2 + c})
+        block = kv_part(j, mine)
+        send(block, block, xsend.at[count + j], kvrecv.at[0, j], to_fore)
+        send(block, block, xsend.at[count + j], kvrecv.at[1, j], to_back)
+        if j > 0:
+            send(block, block, xsend.at[count + j], kvrecv.at[2, j], {"sp": (x + 2) % nx * 2 + c})
+        send(block, block, ssend.at[count + j], kvsib.at[j], to_core)
 
     def kv_pass(j):
-        block = kvbuf.at[j, of_back]
+        block = kv_part(j, of_back)
         arrived(block, kvrecv.at[0, j])
         if j == 0:
-            send(block, block, xsend.at[3 + j], kvrecv.at[2, j], to_fore)
-        send(block, block, ssend.at[3 + j], kvsib.at[j], to_core)
+            send(block, block, xsend.at[count + j], kvrecv.at[2, j], to_fore)
+        send(block, block, ssend.at[count + j], kvsib.at[j], to_core)
 
     def kv_far(j):
         for kind, piece in ((1, of_fore), (2, of_far)):
-            block = kvbuf.at[j, piece]
+            block = kv_part(j, piece)
             arrived(block, kvrecv.at[kind, j])
-            send(block, block, ssend.at[3 + j], kvsib.at[j], to_core)
+            send(block, block, ssend.at[count + j], kvsib.at[j], to_core)
 
     send_own(0)
     send_own(1)
@@ -270,13 +290,15 @@
 
     def early(i):
         norm_block(i)
-        pl.when(i == OFFSETS[2] - 1)(lambda: send_own(2))
+        for m in range(2, count):
+            pl.when(i == OFFSETS[m] - 1)(functools.partial(send_own, m))
 
     done = 1 + rows // norm_rows
     slots(1, done, early)
     for load in loads[2:]:
         load.wait()
-    add_source(2, r)
+    for m in range(2, count):
+        add_source(m, r)
     ends = [nz + at + LAG_F for at in OFFSETS]
     slots(done, ends[0])
     project(0)
@@ -289,14 +311,16 @@
     qbuf[...] = acc[1].astype(jnp.bfloat16)
     send_sums(1, qbuf[...])
     kv_pass(0)
-    slots(ends[1], ends[2] - 1)
+    slots(ends[1], ends[1] + 1)
     kv_far(0)
-    slots(ends[2] - 1, ends[2])
+    slots(ends[1] + 1, ends[1] + 2)
+    kvbuf[1, mine, :, 0:split] = acc[2, :, 0:split].astype(jnp.bfloat16)
+    kv_send(1)
     share_key_scale()
-    slots(ends[2], nz + OFFSETS[2] + LAG_G)
-    kvbuf[1, mine] = acc[2].astype(jnp.bfloat16)
-    kv_send(1)
-    arrived(kvbuf.at[0, pl.ds(0, nx)], kvsib.at[0])
+    slots(ends[1] + 2, nz + OFFSETS[3] + LAG_G)
+    kvbuf[1, mine, :, split:cols] = acc[2, :, split:cols].astype(jnp.bfloat16)
+    kv_send(2)
+    arrived(kv_part(0, pl.ds(0, nx)), kvsib.at[0])
     normalise_keys()
     qbuf[...] = normalise(qbuf[...], inverse_rms(1), qgain_ref)
 
@@ -309,33 +333,36 @@
         weights = jnp.exp(scores - jnp.max(scores, axis=-1, keepdims=True))
         totals.append(jnp.sum(weights, axis=-1, keepdims=True))
         probs[h] = weights.astype(jnp.bfloat16)
-        if h == 0:
-            kv_pass(1)
-            kv_far(1)
-    arrived(kvbuf.at[1, pl.ds(0, nx)], kvsib.at[1])
+        if h < 2:
+            kv_pass(1 + h)
+            kv_far(1 + h)
+    arrived(kv_part(1, pl.ds(0, nx)), kvsib.at[1])
     for h in range(heads):
         at = slice(h * HEAD_DIM, (h + 1) * HEAD_DIM)
+        if h == heads - 1:
+            arrived(kv_part(2, pl.ds(0, nx)), kvsib.at[2])
         context = dot(probs[h], kvbuf[1, :, :, at].reshape(keys_all, HEAD_DIM)) / totals[h]
         out_ref[:, at] = context.astype(jnp.bfloat16)
 
 
-    def pieces(m, count):
-        outer = max(a for a in range(1, nz + 1) if count % a == 0 and count // a <= 2 * nx)
-        return wbuf.at[m, pl.ds(0, outer), pl.ds(0, count // outer)]
-
-    def wait_sends(count):
-        for m in range(3):
-            sent(pieces(m, count * (2 if PAIRS[m] else 1)), zsend.at[m])
+    def pieces(m, copies):
+        outer = max(a for a in range(1, nz + 1) if copies % a == 0 and copies // a <= 2 * nx)
+        return weight(m, pl.ds(0, outer), pl.ds(0, copies // outer))
+
+    def wait_sends(copies):
+        for m in range(count):
+            sent(pieces(m, copies * (2 if PAIRS[m] else 1)), zsend.at[m])
 
     pl.when(edge > 0)(lambda: wait_sends(nz + 1))
     pl.when(edge == 0)(lambda: wait_sends(1))
-    for m in range(3):
+    for m in range(count):
         sent(pieces(m, (nz - 1) * (2 if PAIRS[m] else 3)), xsend.at[m])
-    for m in range(3):
-        sent(wbuf.at[m, pl.ds(0, nz - 1), pl.ds(0, nx)], ssend.at[m])
+    for m in range(count):
+        sent(weight(m, pl.ds(0, nz - 1), pl.ds(0, nx)), ssend.at[m])
+    for j in range(3):
+        sent(kv_part(j, pl.ds(0, 3)), xsend.at[count + j])
+        sent(kv_part(j, pl.ds(0, nx)), ssend.at[count + j])
     for j in range(2):
-        sent(kvbuf.at[j, pl.ds(0, 3)], xsend.at[3 + j])
-        sent(kvbuf.at[j, pl.ds(0, nx)], ssend.at[3 + j])
         sent(sums.at[j, pl.ds(0, nt - 1)], sumsend.at[j])
     sent(scales.at[pl.ds(0, 2 * nx - 1)], scalesend)
 
@@ -368,17 +395,17 @@
             pltpu.VMEM((2 * nx, rows, cols), jnp.bfloat16),
             pltpu.SemaphoreType.REGULAR,
             dma((5,)),
-            dma((3, nz)),
-            dma((3, nz)),
-            dma((3, 3, nz)),
-            dma((3, nz)),
-            dma((3, nz)),
-            dma((2,)),
+            dma((4, nz)),
+            dma((4, nz)),
+            dma((3, 4, nz)),
+            dma((4, nz)),
+            dma((3, 3)),
+            dma((3,)),
             dma((2,)),
             dma,
-            dma((3,)),
-            dma((5,)),
-            dma((5,)),
+            dma((4,)),
+            dma((7,)),
+            dma((7,)),
             dma((2,)),
             dma,
         ],

time: 84.1 us -> 82.3 us (0.979)
  Pallas kernels: 81.6 us -> 79.7 us
    pallas_call x1, Pallas kernels: 81.6 us -> 79.7 us  [local(): pl.pallas_call(functools.partial(kernel, sizes), out_shape=jax.ShapeDtype...]
where the time goes in v6:
time: 82.3 us; the launch traced here: 82 us
  Pallas kernels  79.7 us (97%)
  local copies, waits for them, and re-layouts  1.59 us (2%)
    pallas_call x1, Pallas kernels, local(): pl.pallas_call(functools.partial(kernel, sizes), out_shape=jax.ShapeDtype...  79.7 us

profile of v6, /device:TPU:1, one launch (start us, length us, event | category | flops | bytes accessed | tf_op | source)
XLA Modules:
  0.0 82.0 jit_solution(16589359211422396150)
XLA Ops:
  0.7 79.7 %shard_map.82 = bf16[192,384]{1,0:T(8,128)(2,1)} custom-call(s32[1]{0:T(128)S(6)} %copy.10.steps_ref, bf16[192,5120]{1,0:T(8,128)(2,1)} %bitcast.7, f32[50,2,5120]{2,1,0:T(2,128)} %table_hbm.1, bf16[8,80,384]{2,1,0:T(8,128)(2,1)} %bitcast.9, bf16[8,80,384]{2,1,0:T(8,128)(2,1)} %bitcast.10, bf16[8,80,384]{2,1,0:T(8,128)(2,1)} %bitcast.11, ...), custom_call_target="tpu_custom_call" | custom-call | tf_op jit(solution)/shard_map/pallas_call | solution.py:378
  80.4 1.6 %copy.11 = bf16[1,1,192,384]{3,2,1,0:T(8,128)(2,1)} copy(bf16[1,1,192,384]{3,2,1,0:T(8,128)(2,1)} %bitcast.8) | data formatting | bytes 294912

commit v7 on v6

--- a/solution.py
+++ b/solution.py
@@ -11,8 +11,7 @@
 OFFSETS = (0, 1, 2, 3)
 PAIRS = (False, False, True, True)
 LAG_X = 1
-LAG_F = 2
-LAG_G = 3
+LAG_F = (2, 2, 1, 1)
 MESH = pl.DeviceIdType.MESH
 
 
@@ -49,10 +48,6 @@
         which, first, end = streams[m]
         return wbuf.at[which, src, piece, :, pl.ds(first, end - first)]
 
-    def own_weight(m, piece):
-        which, first, end = streams[m]
-        return whbm[which].at[piece, :, pl.ds(first, end - first)]
-
     shared = ((0, 0, cols), (1, 0, split), (1, split, cols))
 
     def kv_part(j, piece):
@@ -113,9 +108,9 @@
 
     def send_own(m):
         def one(where, way):
-            send(own_weight(m, mine), weight(m, r, mine), zsend.at[m], zrecv.at[m, r], where)
+            send(weight(m, r, mine), weight(m, r, mine), zsend.at[m], zrecv.at[m, r], where)
             if PAIRS[m]:
-                send(own_weight(m, of_far), weight(m, r, of_far), zsend.at[m], zfar.at[m, r], where)
+                send(weight(m, r, of_far), weight(m, r, of_far), zsend.at[m], zfar.at[m, r], where)
         both_ways(one)
 
     def over_sources(k, least, action):
@@ -174,6 +169,9 @@
             to_sibling(m, src)
         nth_source(n, one)
 
+    norm_count = 4
+    norm_rows = rows // norm_count
+
     def add_source(m, src):
         depth = width // nz
         at = pl.ds(pl.multiple_of(src * depth, HEAD_DIM), depth)
@@ -184,8 +182,12 @@
         arrived(weight(m, src, pl.ds(base, nx)), srecv.at[m, src])
         add_source(m, src)
 
+    def use_nth(n, m):
+        nth_source(n, lambda src: use(m, src))
+
     def g_event(n, m):
-        nth_source(n, lambda src: use(m, src))
+        ready = jnp.logical_and(n + OFFSETS[m] + LAG_F[m] + 1 > norm_count, n < nz - 1 if m < 2 else n < nz)
+        pl.when(ready)(lambda: use_nth(n, m))
 
     def slot(t):
         for m in range(count):
@@ -193,9 +195,9 @@
         for m in range(count):
             x_event(t - OFFSETS[m] - LAG_X, m)
         for m in range(count):
-            f_event(t - OFFSETS[m] - LAG_F, m)
-        for m in range(2, count):
-            g_event(t - OFFSETS[m] - LAG_G, m)
+            f_event(t - OFFSETS[m] - LAG_F[m], m)
+        for m in range(count):
+            g_event(t - OFFSETS[m] - LAG_F[m] - 1, m)
 
     def slots(first, end, extra=None):
         @pl.loop(first, end)
@@ -204,7 +206,6 @@
             if extra is not None:
                 extra(t - first)
 
-    norm_rows = rows // 4
 
     def norm_block(i):
         at = pl.ds(pl.multiple_of(i * norm_rows, norm_rows), norm_rows)
@@ -213,12 +214,6 @@
         spread = jnp.mean(center * center, axis=-1, keepdims=True)
         scaled = center * lax.rsqrt(spread + 1e-06) * modulation[1:2, :] + modulation[0:1, :]
         normed[at, :] = scaled.astype(jnp.bfloat16)
-
-    def project(m):
-        @pl.loop(0, nz)
-        def _(src):
-            pl.when(src == r)(lambda: add_source(m, src))
-            pl.when(src != r)(lambda: use(m, src))
 
     def send_sums(i, values):
         wide = values.astype(jnp.float32)
@@ -280,6 +275,8 @@
             arrived(block, kvrecv.at[kind, j])
             send(block, block, ssend.at[count + j], kvsib.at[j], to_core)
 
+    for load in loads[2:]:
+        load.wait()
     send_own(0)
     send_own(1)
     acc[...] = jnp.zeros_like(acc)
@@ -293,31 +290,30 @@
         for m in range(2, count):
             pl.when(i == OFFSETS[m] - 1)(functools.partial(send_own, m))
 
-    done = 1 + rows // norm_rows
+    done = 1 + norm_count
     slots(1, done, early)
-    for load in loads[2:]:
-        load.wait()
-    for m in range(2, count):
+    for m in range(count):
         add_source(m, r)
-    ends = [nz + at + LAG_F for at in OFFSETS]
+        for n in range(1, norm_count - OFFSETS[m] - LAG_F[m]):
+            use_nth(n, m)
+    ends = [nz + at + lag for at, lag in zip(OFFSETS, LAG_F)]
     slots(done, ends[0])
-    project(0)
+    use_nth(nz - 1, 0)
     kvbuf[0, mine] = acc[0].astype(jnp.bfloat16)
     kv_send(0)
     pl.when(lower)(lambda: pl.semaphore_wait(answered, ny))
     send_sums(0, kvbuf[0, mine])
     slots(ends[0], ends[1])
-    project(1)
+    use_nth(nz - 1, 1)
     qbuf[...] = acc[1].astype(jnp.bfloat16)
     send_sums(1, qbuf[...])
     kv_pass(0)
-    slots(ends[1], ends[1] + 1)
-    kv_far(0)
-    slots(ends[1] + 1, ends[1] + 2)
+    slots(ends[1], ends[2] + 1)
     kvbuf[1, mine, :, 0:split] = acc[2, :, 0:split].astype(jnp.bfloat16)
     kv_send(1)
+    kv_far(0)
     share_key_scale()
-    slots(ends[1] + 2, nz + OFFSETS[3] + LAG_G)
+    slots(ends[2] + 1, ends[3] + 1)
     kvbuf[1, mine, :, split:cols] = acc[2, :, split:cols].astype(jnp.bfloat16)
     kv_send(2)
     arrived(kv_part(0, pl.ds(0, nx)), kvsib.at[0])

time: 82.3 us -> 81.5 us (level)
  no operation moved by 1% of the time
where the time goes in v7:
time: 81.5 us; the launch traced here: 81.2 us
  Pallas kernels  79 us (97%)
  local copies, waits for them, and re-layouts  1.59 us (2%)
    pallas_call x1, Pallas kernels, local(): pl.pallas_call(functools.partial(kernel, sizes), out_shape=jax.ShapeDtype...  79 us

profile of v7, /device:TPU:1, one launch (start us, length us, event | category | flops | bytes accessed | tf_op | source)
XLA Modules:
  0.0 81.2 jit_solution(9142422454471629252)
XLA Ops:
  0.7 79.0 %shard_map.82 = bf16[192,384]{1,0:T(8,128)(2,1)} custom-call(s32[1]{0:T(128)S(6)} %copy.10.steps_ref, bf16[192,5120]{1,0:T(8,128)(2,1)} %bitcast.7, f32[50,2,5120]{2,1,0:T(2,128)} %table_hbm.1, bf16[8,80,384]{2,1,0:T(8,128)(2,1)} %bitcast.9, bf16[8,80,384]{2,1,0:T(8,128)(2,1)} %bitcast.10, bf16[8,80,384]{2,1,0:T(8,128)(2,1)} %bitcast.11, ...), custom_call_target="tpu_custom_call" | custom-call | tf_op jit(solution)/shard_map/pallas_call | solution.py:374
  79.6 1.6 %copy.11 = bf16[1,1,192,384]{3,2,1,0:T(8,128)(2,1)} copy(bf16[1,1,192,384]{3,2,1,0:T(8,128)(2,1)} %bitcast.8) | data formatting | bytes 294912

commit v8 on v7

--- a/solution.py
+++ b/solution.py
@@ -66,9 +66,6 @@
     loads = [pltpu.make_async_copy(latents_hbm, latents, local_sem.at[0]),
              pltpu.make_async_copy(table_hbm, table, local_sem.at[1])]
     loads += [pltpu.make_async_copy(whbm[m], wbuf.at[m, r], local_sem.at[2 + m]) for m in range(3)]
-    for load in loads:
-        load.start()
-
     barrier = pltpu.get_barrier_semaphore()
 
     def greet(where):
@@ -94,6 +91,8 @@
         pl.when(lower)(lambda: pl.semaphore_wait(barrier, near))
         pl.when(jnp.logical_not(lower))(lambda: pl.semaphore_wait(barrier, near + ny))
 
+    for load in loads:
+        load.start()
     pl.when(at_end)(lambda: wait_greetings(3 + ny))
     pl.when(jnp.logical_not(at_end))(lambda: wait_greetings(4 + ny))
 
@@ -300,9 +299,9 @@
     slots(done, ends[0])
     use_nth(nz - 1, 0)
     kvbuf[0, mine] = acc[0].astype(jnp.bfloat16)
-    kv_send(0)
     pl.when(lower)(lambda: pl.semaphore_wait(answered, ny))
     send_sums(0, kvbuf[0, mine])
+    kv_send(0)
     slots(ends[0], ends[1])
     use_nth(nz - 1, 1)
     qbuf[...] = acc[1].astype(jnp.bfloat16)

time: 81.5 us -> 81.5 us (level)
  no operation moved by 1% of the time
where the time goes in v8:
time: 81.5 us; the launch traced here: 81.2 us
  Pallas kernels  79 us (97%)
  local copies, waits for them, and re-layouts  1.59 us (2%)
    pallas_call x1, Pallas kernels, local(): pl.pallas_call(functools.partial(kernel, sizes), out_shape=jax.ShapeDtype...  79 us

profile of v8, /device:TPU:1, one launch (start us, length us, event | category | flops | bytes accessed | tf_op | source)
XLA Modules:
  0.0 81.2 jit_solution(2105825462799181456)
XLA Ops:
  0.7 79.0 %shard_map.82 = bf16[192,384]{1,0:T(8,128)(2,1)} custom-call(s32[1]{0:T(128)S(6)} %copy.10.steps_ref, bf16[192,5120]{1,0:T(8,128)(2,1)} %bitcast.7, f32[50,2,5120]{2,1,0:T(2,128)} %table_hbm.1, bf16[8,80,384]{2,1,0:T(8,128)(2,1)} %bitcast.9, bf16[8,80,384]{2,1,0:T(8,128)(2,1)} %bitcast.10, bf16[8,80,384]{2,1,0:T(8,128)(2,1)} %bitcast.11, ...), custom_call_target="tpu_custom_call" | custom-call | tf_op jit(solution)/shard_map/pallas_call | solution.py:373
  79.6 1.6 %copy.11 = bf16[1,1,192,384]{3,2,1,0:T(8,128)(2,1)} copy(bf16[1,1,192,384]{3,2,1,0:T(8,128)(2,1)} %bitcast.8) | data formatting | bytes 294912
